TPU v7x, 32 devices: a whole 2x2x4 slice. The times are simulated.
32 devices in a mesh: dp: 8 (over y, x, core), fsdp: 4 (over z).
Axes of the slice: x: 2, y: 2, z: 4, core: 2. Of those that a mesh axis runs over, the one named last changes fastest.
Arguments:
- activations: bfloat16 [2048, 4096], P('dp', 'fsdp'), may hold values from -6 to 6
- output_grads: bfloat16 [2048, 4096], P('dp', 'fsdp'), may hold values from -6 to 6
- basis: bfloat16 [4096, 1024], P('fsdp'), may hold values from -0.09375 to 0.09375
- weight: bfloat16 [4096, 4096], P('fsdp'), may hold values from -0.09375 to 0.09375
- first_moment: float32 [4096, 1024], P(('fsdp', 'dp')), may hold values from -0.06 to 0.06
- second_moment: float32 [4096, 1024], P(('fsdp', 'dp')), may hold values from 1e-07 to 1e-05
Outputs:
- new_weight: bfloat16 [4096, 4096], P('fsdp')
- new_first: float32 [4096, 1024], P(('fsdp', 'dp'))
- new_second: float32 [4096, 1024], P(('fsdp', 'dp'))
All inputs are finite; a program needn't handle non-finite values.
Results may differ from a plain program's by a relative error of at most 0.0036.
Values may be sent and summed in bfloat16 or wider, within the bound.
A program may use at most 64 MiB of HBM per device.

v0:
```python
import jax
import jax.numpy as jnp
from jax import lax
from jax.sharding import PartitionSpec as P

first_decay = 0.9
second_decay = 0.999
first_fix = 1.0 - 0.9**10
second_fix = 1.0 - 0.999**10
step_rate = 0.01
tiny_eps = 1e-08


def times_basis(update, rows):
    return lax.dot_general(
        update, rows, (((1,), (1,)), ((), ())), preferred_element_type=jnp.float32
    )


def local(activations, output_grads, basis, weight, first_moment, second_moment):
    partial_product = jnp.dot(activations, basis, preferred_element_type=jnp.float32)
    projected = lax.psum(partial_product, "fsdp").astype(jnp.bfloat16)
    total_tokens = projected.shape[0] * lax.axis_size("dp")
    local_term = (
        lax.dot_general(
            output_grads, projected, (((0,), (0,)), ((), ())), preferred_element_type=jnp.float32
        )
        / total_tokens
    )
    low_grad = lax.psum_scatter(local_term, "dp", scatter_dimension=0, tiled=True)
    new_first = first_decay * first_moment + (1.0 - first_decay) * low_grad
    new_second = second_decay * second_moment + (1.0 - second_decay) * low_grad * low_grad
    update = (new_first / first_fix / (jnp.sqrt(new_second / second_fix) + tiny_eps)).astype(
        jnp.bfloat16
    )
    all_updates = lax.all_gather(update, "dp", axis=0, tiled=True)
    decoded = times_basis(all_updates, lax.all_gather(basis, "fsdp", axis=0, tiled=True))
    new_weight = (weight.astype(jnp.float32) - step_rate * decoded).astype(jnp.bfloat16)
    return (new_weight, new_first, new_second)


def solution(mesh):
    return jax.shard_map(
        local,
        mesh=mesh,
        in_specs=(
            P("dp", "fsdp"),
            P("dp", "fsdp"),
            P("fsdp", None),
            P("fsdp", None),
            P(("fsdp", "dp"), None),
            P(("fsdp", "dp"), None),
        ),
        out_specs=(P("fsdp", None), P(("fsdp", "dp"), None), P(("fsdp", "dp"), None)),
        check_vma=False,
    )
```

profile of v0, /device:TPU:0, one launch (start us, length us, event | category | flops | bytes accessed | tf_op | source)
XLA Modules:
  0.0 313.4 jit_solution(17519552105891862201)
XLA Ops:
  7.2 0.0 copy-start
  7.2 0.0 copy-start.1
  7.2 0.0 reduce-scatter.2.cloned.1.call-start
  7.2 2.5 fusion.3
  9.8 0.0 copy-start.2
  9.8 45.3 %all-reduce.1 = bf16[256,1024]{1,0:T(8,128)(2,1)S(1)} all-reduce(f32[256,1024]{1,0:T(8,128)S(1)} %fusion.3), channel_id=1, replica_groups=mesh['dp'=8,'fsdp'=4] {'fsdp'}, use_global_device_ids=true, to_apply=%region_0.0 | all-reduce | flops 262144 | bytes 1572864 | tf_op jit(solution)/shard_map/psum | solution.py:22
  55.1 0.0 copy-done
  55.1 2.8 multiply_bitcast_fusion
  57.8 0.0 reduce-scatter.2.cloned.1.call-update
  57.9 0.0 all-gather.3.cloned.1.call-start
  57.9 0.0 copy-done.1
  57.9 0.2 copy.9
  58.1 0.0 copy-done.2
  58.1 0.2 copy.10
  58.3 50.2 %reduce-scatter.2.cloned.1.call-done = f32[128,1024]{0,1:T(8,128)} async-done(((f32[1024,1024]{0,1:T(8,128)}), f32[128,1024]{0,1:T(8,128)}) %reduce-scatter.2.cloned.1.call-update) | async-done | bytes 524304 | tf_op jit(solution)/shard_map/reduce_scatter | solution.py:30
  108.5 2.1 divide_convert_fusion
  110.6 0.0 all-gather.3.cloned.1.call-update
  110.7 0.0 all-gather.5.cloned.1.call-start
  110.7 0.7 all-gather.5.cloned.1.call-update
  111.4 1.0 copy.11
  112.4 1.0 copy.12
  113.4 26.0 %all-gather.3.cloned.1.call-done = bf16[1024,1024]{0,1:T(8,128)(2,1)} async-done(((bf16[128,1024]{0,1:T(8,128)(2,1)}), bf16[1024,1024]{0,1:T(8,128)(2,1)}) %all-gather.3.cloned.1.call-update) | async-done | bytes 2097168 | tf_op jit(solution)/shard_map/all_gather | solution.py:36
  139.4 151.3 %all-gather.5.cloned.1.call-done = bf16[4096,1024]{1,0:T(8,128)(2,1)} async-done(((bf16[1024,1024]{1,0:T(8,128)(2,1)}), bf16[4096,1024]{1,0:T(8,128)(2,1)}) %all-gather.5.cloned.1.call-update) | async-done | bytes 8388624 | tf_op jit(solution)/shard_map/all_gather | solution.py:37
  290.7 16.2 %subtract_convert_fusion = bf16[1024,4096]{1,0:T(8,128)(2,1)} fusion(bf16[1024,4096]{1,0:T(8,128)(2,1)} %param.9, bf16[1024,1024]{0,1:T(8,128)(2,1)} %all-gather.3.cloned.1.call-done, bf16[4096,1024]{1,0:T(8,128)(2,1)} %all-gather.5.cloned.1.call-done), kind=kOutput, calls=%fused_computation | convolution fusion | flops 8606711808 | bytes 27262976 | tf_op jit(solution)/shard_map/dot_general | solution.py:15
Async XLA Ops:
  7.2 47.9 %copy-start = (bf16[256,1024]{1,0:T(8,128)(2,1)S(1)}, bf16[256,1024]{1,0:T(8,128)(2,1)}, u32[]{:S(2)}) copy-start(bf16[256,1024]{1,0:T(8,128)(2,1)} %param.7) | copy-start | bytes 1572868
  7.2 50.7 %copy-start.1 = (f32[128,1024]{1,0:T(8,128)S(1)}, f32[128,1024]{1,0:T(8,128)}, u32[]{:S(2)}) copy-start(f32[128,1024]{1,0:T(8,128)} %param.10) | copy-start | bytes 1572868
  7.2 101.4 %reduce-scatter.2.cloned.1.call-start = ((), (), s32[]{:S(2)}) async-start(), calls=%async_computation.1 | async-start | bytes 4718592 | tf_op jit(solution)/shard_map/reduce_scatter | solution.py:30
  9.8 48.3 %copy-start.2 = (f32[128,1024]{1,0:T(8,128)S(1)}, f32[128,1024]{1,0:T(8,128)}, u32[]{:S(2)}) copy-start(f32[128,1024]{1,0:T(8,128)} %param.11) | copy-start | bytes 1572868
  57.9 81.5 %all-gather.3.cloned.1.call-start = ((), (), s32[]{:S(2)}) async-start(), calls=%async_computation.2 | async-start | bytes 2359296 | tf_op jit(solution)/shard_map/all_gather | solution.py:36
  110.7 180.0 %all-gather.5.cloned.1.call-start = ((), (), s32[]{:S(2)}) async-start(), calls=%async_computation.3 | async-start | bytes 10485760 | tf_op jit(solution)/shard_map/all_gather | solution.py:37
Sparse Core Ops, SparseCore 0:
  58.0 50.5 reduce-scatter.1
  111.1 28.1 all-gather.2
  141.0 149.6 all-gather.4
where the time goes:
time: 314 us; the launch traced here: 313 us
  waiting for transfers between devices  228 us (73%)
  blocking collectives  45.3 us (14%)
  matrix products  21.5 us (7%)
  between operations  13.8 us (4%)
    all_gather x1, waiting for transfers between devices, local(): lax.all_gather(basis, 'fsdp', axis=0, tiled=True)  151 us
    reduce_scatter x1, waiting for transfers between devices, local(): lax.psum_scatter(local_term, 'dp', scatter_dimension=0, tiled=True)  50.2 us
    psum x1, blocking collectives, local(): projected = lax.psum(partial_product, 'fsdp').astype(jnp.bfloat16)  45.3 us
    all_gather x1, waiting for transfers between devices, local(): all_updates = lax.all_gather(update, 'dp', axis=0, tiled=True)  26 us
    dot_general x1, matrix products, times_basis(): lax.dot_general(update, rows, (((1,), (1,)), ((), ())), preferred_element...  16.2 us
  transfers between devices with their start and end apart: 3, of which 3 were waited for; matrix products, arithmetic and copies ran while one was open for 1% of the time, Pallas kernels for 0%

commit v1 on v0

v1 whole, which is shorter than its diff:
```python
import functools

import jax
import jax.numpy as jnp
from jax import lax
from jax.experimental import pallas as pl
from jax.experimental.pallas import tpu as pltpu
from jax.sharding import PartitionSpec as P

first_decay = 0.9
second_decay = 0.999
first_fix = 1.0 - 0.9**10
second_fix = 1.0 - 0.999**10
step_rate = 0.01
tiny_eps = 1e-08
MESH = pl.DeviceIdType.MESH
f32 = jnp.float32
bf16 = jnp.bfloat16


def times_basis(update, rows):
    return lax.dot_general(update, rows, (((1,), (1,)), ((), ())), preferred_element_type=f32)


def adam(first, second, low_grad):
    new_first = first_decay * first + (1.0 - first_decay) * low_grad
    new_second = second_decay * second + (1.0 - second_decay) * low_grad * low_grad
    update = (new_first / first_fix / (jnp.sqrt(new_second / second_fix) + tiny_eps)).astype(bf16)
    return new_first, new_second, update


def exchange_kernel(
    act, og, basis, first, second,
    updates, rows_out, new_first, new_second,
    part, part_send, part_recv, proj,
    grad, grad_core, sa1, sb1, ra1, rb1, sa2, sb2, ra2, rb2,
    own_sem, z_send, z_fwd, z_recv, rs_send, rs_recv, ag_send, ag_recv,
    core_send, core_recv, h1_send, h1_recv, h2_send, h2_recv, pg_send, pg_recv,
):
    i = lax.axis_index("dp")
    j = lax.axis_index("fsdp")
    ndp, nf = 8, 4
    core, x, y = i % 2, (i // 2) % 2, i // 4
    sib = i + 1 - 2 * core
    xn = i + 2 * (1 - 2 * x)
    yn = i + 4 * (1 - 2 * y)
    dn = xn + 4 * (1 - 2 * y)
    tokens, rank = act.shape[0], first.shape[1]
    own_rows = first.shape[0]
    tb = tokens // nf
    half = rank // 2
    total_tokens = tokens * ndp

    def remote(src, dst, ssem, rsem, dp, z):
        return pltpu.make_async_remote_copy(
            src_ref=src, dst_ref=dst, send_sem=ssem, recv_sem=rsem,
            device_id=(dp, z), device_id_type=MESH,
        )

    def got(dst, rsem, ssem):
        remote(dst, dst, ssem, rsem, sib, j).wait_recv()

    def sent(src, ssem, rsem):
        remote(src, src, ssem, rsem, sib, j).wait_send()

    barrier = pltpu.get_barrier_semaphore()
    for dp in (sib, xn, yn):
        pl.semaphore_signal(barrier, inc=1, device_id=(dp, j), device_id_type=MESH)
    for d in range(1, nf):
        pl.semaphore_signal(barrier, inc=1, device_id=(i, (j + d) % nf), device_id_type=MESH)
    pl.semaphore_wait(barrier, 3 + nf - 1)

    own_copy = pltpu.make_async_copy(basis, rows_out.at[pl.ds(j * ndp, ndp)], own_sem)
    own_copy.start()

    def z_piece(shard):
        return rows_out.at[shard * ndp + i]

    @pl.when(j < nf - 1)
    def _():
        remote(basis.at[i], z_piece(j), z_send.at[0], z_recv.at[j], i, j + 1).start()

    @pl.when(j > 0)
    def _():
        remote(basis.at[i], z_piece(j), z_send.at[1], z_recv.at[j], i, j - 1).start()

    a = act[...]
    acc = None
    for k in range(ndp):
        term = jnp.dot(a[:, k * own_rows : (k + 1) * own_rows], basis[k], preferred_element_type=f32)
        acc = term if acc is None else acc + term
    part[...] = acc.reshape(nf, tb, rank)
    part_send[...] = acc.reshape(nf, tb, rank).astype(bf16)
    for d in (1, 2, 3):
        z = (j + d) % nf
        remote(part_send.at[z], part_recv.at[j], rs_send.at[z], rs_recv.at[j], i, z).start()

    def block(buf, base, k):
        return buf.at[base + k]

    def lane_a(buf, base, k):
        return buf.at[base + k, :, pl.ds(0, half)]

    def lane_b(buf, base, k):
        return buf.at[base + k, :, pl.ds(half, half)]

    def stage1(buf, base, g):
        mine = block(buf, base, i)
        remote(mine, mine, pg_send.at[g, 0], pg_recv.at[g, 0], xn, j).start()
        remote(mine, mine, pg_send.at[g, 1], pg_recv.at[g, 1], yn, j).start()
        remote(mine, mine, pg_send.at[g, 4], pg_recv.at[g, 4], sib, j).start()

    def stage2(buf, base, g):
        bx, by = block(buf, base, xn), block(buf, base, yn)
        got(bx, pg_recv.at[g, 0], pg_send.at[g, 0])
        lb = lane_b(buf, base, xn)
        remote(lb, lb, pg_send.at[g, 3], pg_recv.at[g, 3], yn, j).start()
        remote(bx, bx, pg_send.at[g, 5], pg_recv.at[g, 5], sib, j).start()
        got(by, pg_recv.at[g, 1], pg_send.at[g, 1])
        la = lane_a(buf, base, yn)
        remote(la, la, pg_send.at[g, 2], pg_recv.at[g, 2], xn, j).start()
        remote(by, by, pg_send.at[g, 6], pg_recv.at[g, 6], sib, j).start()

    def stage3(buf, base, g):
        got(lane_a(buf, base, dn), pg_recv.at[g, 2], pg_send.at[g, 2])
        got(lane_b(buf, base, dn), pg_recv.at[g, 3], pg_send.at[g, 3])
        bd = block(buf, base, dn)
        remote(bd, bd, pg_send.at[g, 7], pg_recv.at[g, 7], sib, j).start()

    def stage4(buf, base, g):
        for q in range(4):
            o = (i, xn, yn, dn)[q]
            so = o + 1 - 2 * core
            got(block(buf, base, so), pg_recv.at[g, 4 + q], pg_send.at[g, 4 + q])
            sent(block(buf, base, o), pg_send.at[g, 4 + q], pg_recv.at[g, 4 + q])
        sent(block(buf, base, i), pg_send.at[g, 0], pg_recv.at[g, 0])
        sent(block(buf, base, i), pg_send.at[g, 1], pg_recv.at[g, 1])
        sent(lane_a(buf, base, yn), pg_send.at[g, 2], pg_recv.at[g, 2])
        sent(lane_b(buf, base, xn), pg_send.at[g, 3], pg_recv.at[g, 3])

    low = 1 - j // 2
    edge = low * j + (1 - low) * (nf - 1 - j)

    def shard_of(g):
        place = g + (g + nf - edge) // nf
        return low * place + (1 - low) * (nf - 1 - place)

    def basis_in(g):
        s = shard_of(g)
        got(z_piece(s), z_recv.at[s], z_send.at[0])

        @pl.when((s < j) & (j < nf - 1))
        def _():
            remote(z_piece(s), z_piece(s), z_fwd.at[g], z_recv.at[s], i, j + 1).start()

        @pl.when((s > j) & (j > 0))
        def _():
            remote(z_piece(s), z_piece(s), z_fwd.at[g], z_recv.at[s], i, j - 1).start()

        stage1(rows_out, s * ndp, g)

    def basis_sent(g):
        s = shard_of(g)

        @pl.when(((s < j) & (j < nf - 1)) | ((s > j) & (j > 0)))
        def _():
            sent(z_piece(s), z_fwd.at[g], z_recv.at[s])

    basis_in(0)

    total = part[j]
    for d in (1, 2, 3):
        z = (j + d) % nf
        got(part_recv.at[z], rs_recv.at[z], rs_send.at[z])
        total = total + part_recv[z].astype(f32)
    proj[j] = total.astype(bf16)
    for d in (1, 2, 3):
        z = (j + d) % nf
        remote(proj.at[j], proj.at[j], ag_send.at[z], ag_recv.at[j], i, z).start()

    basis_in(1)
    stage2(rows_out, shard_of(0) * ndp, 0)

    for d in (1, 2, 3):
        z = (j + d) % nf
        got(proj.at[z], ag_recv.at[z], ag_send.at[z])

    projected = proj[...].reshape(tokens, rank)

    def term(k):
        cols = pl.ds(pl.multiple_of(k * own_rows, own_rows), own_rows)
        return lax.dot_general(
            og[:, cols], projected, (((0,), (0,)), ((), ())), preferred_element_type=f32
        ) / total_tokens

    for q in range(4):
        grad[4 + q] = term(2 * q + 1 - core)
        remote(grad.at[4 + q], grad_core.at[q], core_send.at[q], core_recv.at[q], sib, j).start()
    for q in range(4):
        grad[q] = term(2 * q + core)
    for q in range(4):
        got(grad_core.at[q], core_recv.at[q], core_send.at[q])
        grad[q] = grad[q] + grad_core[q]

    for n, far in enumerate((1, 0)):
        yy = far * (1 - y) + (1 - far) * y
        sa1[n] = grad[2 * yy + 1 - x, :, 0:half].astype(bf16)
        remote(sa1.at[n], ra1.at[n], h1_send.at[n], h1_recv.at[n], xn, j).start()
        xx = far * (1 - x) + (1 - far) * x
        sb1[n] = grad[2 * (1 - y) + xx, :, half:rank].astype(bf16)
        remote(sb1.at[n], rb1.at[n], h1_send.at[2 + n], h1_recv.at[2 + n], yn, j).start()
    got(ra1.at[0], h1_recv.at[0], h1_send.at[0])
    sa2[...] = grad[2 * (1 - y) + x, :, 0:half] + ra1[0].astype(f32)
    remote(sa2, ra2, h2_send.at[0], h2_recv.at[0], yn, j).start()
    got(rb1.at[0], h1_recv.at[2], h1_send.at[2])
    sb2[...] = grad[2 * y + 1 - x, :, half:rank] + rb1[0].astype(f32)
    remote(sb2, rb2, h2_send.at[1], h2_recv.at[1], xn, j).start()
    got(ra1.at[1], h1_recv.at[1], h1_send.at[1])
    got(rb1.at[1], h1_recv.at[3], h1_send.at[3])

    mine = 2 * y + x
    got(ra2, h2_recv.at[0], h2_send.at[0])
    nf_a, ns_a, up_a = adam(
        first[:, 0:half], second[:, 0:half], grad[mine, :, 0:half] + ra1[1].astype(f32) + ra2[...]
    )
    new_first[:, 0:half] = nf_a
    new_second[:, 0:half] = ns_a
    updates[i, :, 0:half] = up_a
    got(rb2, h2_recv.at[1], h2_send.at[1])
    nf_b, ns_b, up_b = adam(
        first[:, half:rank], second[:, half:rank], grad[mine, :, half:rank] + rb1[1].astype(f32) + rb2[...]
    )
    new_first[:, half:rank] = nf_b
    new_second[:, half:rank] = ns_b
    updates[i, :, half:rank] = up_b
    stage1(updates, 0, 3)

    basis_in(2)
    stage2(rows_out, shard_of(1) * ndp, 1)
    stage3(rows_out, shard_of(0) * ndp, 0)
    stage2(updates, 0, 3)
    stage3(rows_out, shard_of(1) * ndp, 1)
    stage2(rows_out, shard_of(2) * ndp, 2)
    stage3(updates, 0, 3)
    stage3(rows_out, shard_of(2) * ndp, 2)
    for g in range(3):
        stage4(rows_out, shard_of(g) * ndp, g)
        basis_sent(g)
    stage4(updates, 0, 3)

    own_copy.wait()

    @pl.when(j < nf - 1)
    def _():
        sent(basis.at[i], z_send.at[0], z_recv.at[j])

    @pl.when(j > 0)
    def _():
        sent(basis.at[i], z_send.at[1], z_recv.at[j])

    for d in (1, 2, 3):
        z = (j + d) % nf
        sent(part_send.at[z], rs_send.at[z], rs_recv.at[z])
        sent(proj.at[j], ag_send.at[z], ag_recv.at[z])
    for q in range(4):
        sent(grad.at[4 + q], core_send.at[q], core_recv.at[q])
    for n in range(2):
        sent(sa1.at[n], h1_send.at[n], h1_recv.at[n])
        sent(sb1.at[n], h1_send.at[2 + n], h1_recv.at[2 + n])
    sent(sa2, h2_send.at[0], h2_recv.at[0])
    sent(sb2, h2_send.at[1], h2_recv.at[1])


def local_fused(activations, output_grads, basis, weight, first_moment, second_moment):
    tokens, _ = activations.shape
    shard_rows, rank = basis.shape
    own_rows = first_moment.shape[0]
    ndp, nf = lax.axis_size("dp"), lax.axis_size("fsdp")
    half = rank // 2
    vmem = pl.BlockSpec(memory_space=pltpu.VMEM)
    dma = pltpu.SemaphoreType.DMA
    updates, rows, new_first, new_second = pl.pallas_call(
        exchange_kernel,
        out_shape=(
            jax.ShapeDtypeStruct((ndp, own_rows, rank), bf16),
            jax.ShapeDtypeStruct((nf * ndp, own_rows, rank), bf16),
            jax.ShapeDtypeStruct((own_rows, rank), f32),
            jax.ShapeDtypeStruct((own_rows, rank), f32),
        ),
        in_specs=[vmem] * 5,
        out_specs=(vmem, pl.BlockSpec(memory_space=pl.ANY), vmem, vmem),
        scratch_shapes=[
            pltpu.VMEM((nf, tokens // nf, rank), f32),
            pltpu.VMEM((nf, tokens // nf, rank), bf16),
            pltpu.VMEM((nf, tokens // nf, rank), bf16),
            pltpu.VMEM((nf, tokens // nf, rank), bf16),
            pltpu.VMEM((ndp, own_rows, rank), f32),
            pltpu.VMEM((ndp // 2, own_rows, rank), f32),
            pltpu.VMEM((2, own_rows, half), bf16),
            pltpu.VMEM((2, own_rows, half), bf16),
            pltpu.VMEM((2, own_rows, half), bf16),
            pltpu.VMEM((2, own_rows, half), bf16),
            pltpu.VMEM((own_rows, half), f32),
            pltpu.VMEM((own_rows, half), f32),
            pltpu.VMEM((own_rows, half), f32),
            pltpu.VMEM((own_rows, half), f32),
            dma, dma((2,)), dma((3,)), dma((nf,)), dma((nf,)), dma((nf,)), dma((nf,)), dma((nf,)),
            dma((4,)), dma((4,)), dma((4,)), dma((4,)), dma((2,)), dma((2,)), dma((4, 8)), dma((4, 8)),
        ],
        compiler_params=pltpu.CompilerParams(
            collective_id=0, has_side_effects=True, vmem_limit_bytes=48 * 1024 * 1024
        ),
        cost_estimate=pl.CostEstimate(
            flops=4 * tokens * shard_rows * rank, bytes_accessed=24 * 1024 * 1024, transcendentals=0
        ),
    )(
        activations, output_grads, basis.reshape(ndp, own_rows, rank), first_moment, second_moment
    )
    decoded = times_basis(updates.reshape(shard_rows, rank), rows.reshape(nf * shard_rows, rank))
    new_weight = (weight.astype(f32) - step_rate * decoded).astype(bf16)
    return (new_weight, new_first, new_second)


def local(activations, output_grads, basis, weight, first_moment, second_moment):
    partial_product = jnp.dot(activations, basis, preferred_element_type=f32)
    projected = lax.psum(partial_product, "fsdp").astype(bf16)
    total_tokens = projected.shape[0] * lax.axis_size("dp")
    local_term = (
        lax.dot_general(
            output_grads, projected, (((0,), (0,)), ((), ())), preferred_element_type=f32
        )
        / total_tokens
    )
    low_grad = lax.psum_scatter(local_term, "dp", scatter_dimension=0, tiled=True)
    new_first, new_second, update = adam(first_moment, second_moment, low_grad)
    all_updates = lax.all_gather(update, "dp", axis=0, tiled=True)
    decoded = times_basis(all_updates, lax.all_gather(basis, "fsdp", axis=0, tiled=True))
    new_weight = (weight.astype(f32) - step_rate * decoded).astype(bf16)
    return (new_weight, new_first, new_second)


def solution(mesh):
    fused = mesh.shape["dp"] == 8 and mesh.shape["fsdp"] == 4
    return jax.shard_map(
        local_fused if fused else local,
        mesh=mesh,
        in_specs=(
            P("dp", "fsdp"),
            P("dp", "fsdp"),
            P("fsdp", None),
            P("fsdp", None),
            P(("fsdp", "dp"), None),
            P(("fsdp", "dp"), None),
        ),
        out_specs=(P("fsdp", None), P(("fsdp", "dp"), None), P(("fsdp", "dp"), None)),
        check_vma=False,
    )
```

time: 314 us -> 108 us (0.34)
  waiting for transfers between devices: 228 us -> 0 us
  Pallas kernels: 0 us -> 85.6 us
  blocking collectives: 45.3 us -> 0 us
  between operations: 13.8 us -> 0.65 us
  matrix products: 21.5 us -> 15.2 us
  local copies, waits for them, and re-layouts: 2.39 us -> 5.74 us
    all_gather x2 -> x0, waiting for transfers between devices: 177 us -> none  [the longest x1 151 us: local(): lax.all_gather(basis, 'fsdp', axis=0, tiled=True)]
    pallas_call x0 -> x1, Pallas kernels: none -> 85.6 us  [local_fused(): pl.pallas_call(exchange_kernel, out_shape=(jax.ShapeDtypeStruct((ndp, own...]
    reduce_scatter x1 -> x0, waiting for transfers between devices: 50.2 us -> none  [local(): lax.psum_scatter(local_term, 'dp', scatter_dimension=0, tiled=True)]
    psum x1 -> x0, blocking collectives: 45.3 us -> none  [local(): projected = lax.psum(partial_product, 'fsdp').astype(jnp.bfloat16)]
    dot_general x2 -> x0, matrix products: 5.29 us -> none  [the longest x1 2.76 us: local(): lax.dot_general(output_grads, projected, (((0,), (0,)), ((), ())), prefer...]
    unnamed x10, local copies, waits for them, and re-layouts: 2.39 us -> 5.74 us
  transfers between devices with their start and end apart: 3 -> 0, of which waited for: 3 -> 0; matrix products, arithmetic and copies ran while one was open for 1% -> 0% of each run, Pallas kernels for 0% -> 0%
where the time goes in v1:
time: 108 us; the launch traced here: 107 us
  Pallas kernels  85.6 us (79%)
  matrix products  15.2 us (14%)
  local copies, waits for them, and re-layouts  5.74 us (5%)
    pallas_call x1, Pallas kernels, local_fused(): pl.pallas_call(exchange_kernel, out_shape=(jax.ShapeDtypeStruct((ndp, own...  85.6 us
    dot_general x1, matrix products, times_basis(): lax.dot_general(update, rows, (((1,), (1,)), ((), ())), preferred_element...  15.2 us
    unnamed x10, local copies, waits for them, and re-layouts  5.74 us

profile of v1, /device:TPU:0, one launch (start us, length us, event | category | flops | bytes accessed | tf_op | source)
XLA Modules:
  0.0 107.2 jit_solution(7363140336546896570)
XLA Ops:
  0.6 0.0 copy-start
  0.6 1.0 copy-done
  1.7 0.0 copy-start.1
  1.7 1.0 copy-done.1
  2.7 0.0 copy-start.2
  2.7 1.0 copy-done.2
  3.8 0.0 copy-start.3
  3.8 1.0 copy-done.3
  4.8 85.6 %shard_map.85 = (bf16[8,128,1024]{2,1,0:T(8,128)(2,1)S(1)}, bf16[32,128,1024]{2,1,0:T(8,128)(2,1)}, f32[128,1024]{1,0:T(8,128)S(1)}, f32[128,1024]{1,0:T(8,128)S(1)}) custom-call(bf16[256,1024]{1,0:T(8,128)(2,1)S(1)} %copy-done, bf16[256,1024]{1,0:T(8,128)(2,1)S(1)} %copy-done.1, bf16[8,128,1024]{2,1,0:T(8,128)(2,1)} %bitcast.6, f32[128,1024]{1,0:T(8,128)S(1)} %copy-done.2, ...), custom_call_target="tpu_custom_call" | custom-call | flops 1073741824 | bytes 25165824 | tf_op jit(solution)/shard_map/pallas_call | solution.py:282
  90.4 15.2 %subtract_convert_fusion = bf16[1024,4096]{1,0:T(8,128)(2,1)} fusion(bf16[1024,4096]{1,0:T(8,128)(2,1)} %param.9, bf16[1024,1024]{1,0:T(8,128)(2,1)S(1)} %bitcast.5, bf16[4096,1024]{1,0:T(8,128)(2,1)} %bitcast.7), kind=kOutput, calls=%fused_computation | convolution fusion | flops 8606711808 | bytes 27262976 | tf_op jit(solution)/shard_map/dot_general | solution.py:22
  105.6 0.8 copy.11
  106.4 0.8 copy.12
Async XLA Ops:
  0.6 1.0 copy-start
  1.7 1.0 copy-start.1
  2.7 1.0 copy-start.2
  3.8 1.0 copy-start.3

commit v2 on v1

--- a/solution.py
+++ b/solution.py
@@ -29,12 +29,13 @@
     return new_first, new_second, update
 
 
-def exchange_kernel(
-    act, og, basis, first, second,
-    updates, rows_out, new_first, new_second,
+def fused_kernel(
+    act_in, og_in, basis_in_ref, weight_in, first_in, second_in,
+    weight_out, first_out, second_out,
+    act, og, rows, weight, first, second, updates,
     part, part_send, part_recv, proj,
     grad, grad_core, sa1, sb1, ra1, rb1, sa2, sb2, ra2, rb2,
-    own_sem, z_send, z_fwd, z_recv, rs_send, rs_recv, ag_send, ag_recv,
+    load_sem, store_sem, z_send, z_fwd, z_recv, rs_send, rs_recv, ag_send, ag_recv,
     core_send, core_recv, h1_send, h1_recv, h2_send, h2_recv, pg_send, pg_recv,
 ):
     i = lax.axis_index("dp")
@@ -51,6 +52,20 @@
     half = rank // 2
     total_tokens = tokens * ndp
 
+    loads = [
+        pltpu.make_async_copy(src, dst, load_sem.at[n])
+        for n, (src, dst) in enumerate((
+            (act_in, act),
+            (basis_in_ref, rows.at[pl.ds(j * ndp, ndp)]),
+            (og_in, og),
+            (first_in, first),
+            (second_in, second),
+            (weight_in, weight),
+        ))
+    ]
+    for load in loads:
+        load.start()
+
     def remote(src, dst, ssem, rsem, dp, z):
         return pltpu.make_async_remote_copy(
             src_ref=src, dst_ref=dst, send_sem=ssem, recv_sem=rsem,
@@ -70,24 +85,23 @@
         pl.semaphore_signal(barrier, inc=1, device_id=(i, (j + d) % nf), device_id_type=MESH)
     pl.semaphore_wait(barrier, 3 + nf - 1)
 
-    own_copy = pltpu.make_async_copy(basis, rows_out.at[pl.ds(j * ndp, ndp)], own_sem)
-    own_copy.start()
-
     def z_piece(shard):
-        return rows_out.at[shard * ndp + i]
+        return rows.at[shard * ndp + i]
 
     @pl.when(j < nf - 1)
     def _():
-        remote(basis.at[i], z_piece(j), z_send.at[0], z_recv.at[j], i, j + 1).start()
+        remote(basis_in_ref.at[i], z_piece(j), z_send.at[0], z_recv.at[j], i, j + 1).start()
 
     @pl.when(j > 0)
     def _():
-        remote(basis.at[i], z_piece(j), z_send.at[1], z_recv.at[j], i, j - 1).start()
-
+        remote(basis_in_ref.at[i], z_piece(j), z_send.at[1], z_recv.at[j], i, j - 1).start()
+
+    loads[0].wait()
+    loads[1].wait()
     a = act[...]
     acc = None
     for k in range(ndp):
-        term = jnp.dot(a[:, k * own_rows : (k + 1) * own_rows], basis[k], preferred_element_type=f32)
+        term = jnp.dot(a[:, k * own_rows : (k + 1) * own_rows], rows[j * ndp + k], preferred_element_type=f32)
         acc = term if acc is None else acc + term
     part[...] = acc.reshape(nf, tb, rank)
     part_send[...] = acc.reshape(nf, tb, rank).astype(bf16)
@@ -127,11 +141,12 @@
         bd = block(buf, base, dn)
         remote(bd, bd, pg_send.at[g, 7], pg_recv.at[g, 7], sib, j).start()
 
-    def stage4(buf, base, g):
+    def stage4(buf, base, g, receive=True):
         for q in range(4):
             o = (i, xn, yn, dn)[q]
             so = o + 1 - 2 * core
-            got(block(buf, base, so), pg_recv.at[g, 4 + q], pg_send.at[g, 4 + q])
+            if receive:
+                got(block(buf, base, so), pg_recv.at[g, 4 + q], pg_send.at[g, 4 + q])
             sent(block(buf, base, o), pg_send.at[g, 4 + q], pg_recv.at[g, 4 + q])
         sent(block(buf, base, i), pg_send.at[g, 0], pg_recv.at[g, 0])
         sent(block(buf, base, i), pg_send.at[g, 1], pg_recv.at[g, 1])
@@ -157,7 +172,7 @@
         def _():
             remote(z_piece(s), z_piece(s), z_fwd.at[g], z_recv.at[s], i, j - 1).start()
 
-        stage1(rows_out, s * ndp, g)
+        stage1(rows, s * ndp, g)
 
     def basis_sent(g):
         s = shard_of(g)
@@ -178,13 +193,16 @@
         z = (j + d) % nf
         remote(proj.at[j], proj.at[j], ag_send.at[z], ag_recv.at[j], i, z).start()
 
+    stage2(rows, shard_of(0) * ndp, 0)
     basis_in(1)
-    stage2(rows_out, shard_of(0) * ndp, 0)
+    stage3(rows, shard_of(0) * ndp, 0)
+    stage2(rows, shard_of(1) * ndp, 1)
 
     for d in (1, 2, 3):
         z = (j + d) % nf
         got(proj.at[z], ag_recv.at[z], ag_send.at[z])
 
+    loads[2].wait()
     projected = proj[...].reshape(tokens, rank)
 
     def term(k):
@@ -196,6 +214,7 @@
     for q in range(4):
         grad[4 + q] = term(2 * q + 1 - core)
         remote(grad.at[4 + q], grad_core.at[q], core_send.at[q], core_recv.at[q], sib, j).start()
+    basis_in(2)
     for q in range(4):
         grad[q] = term(2 * q + core)
     for q in range(4):
@@ -209,6 +228,7 @@
         xx = far * (1 - x) + (1 - far) * x
         sb1[n] = grad[2 * (1 - y) + xx, :, half:rank].astype(bf16)
         remote(sb1.at[n], rb1.at[n], h1_send.at[2 + n], h1_recv.at[2 + n], yn, j).start()
+    stage3(rows, shard_of(1) * ndp, 1)
     got(ra1.at[0], h1_recv.at[0], h1_send.at[0])
     sa2[...] = grad[2 * (1 - y) + x, :, 0:half] + ra1[0].astype(f32)
     remote(sa2, ra2, h2_send.at[0], h2_recv.at[0], yn, j).start()
@@ -218,45 +238,72 @@
     got(ra1.at[1], h1_recv.at[1], h1_send.at[1])
     got(rb1.at[1], h1_recv.at[3], h1_send.at[3])
 
+    stage2(rows, shard_of(2) * ndp, 2)
     mine = 2 * y + x
+    loads[3].wait()
+    loads[4].wait()
     got(ra2, h2_recv.at[0], h2_send.at[0])
     nf_a, ns_a, up_a = adam(
         first[:, 0:half], second[:, 0:half], grad[mine, :, 0:half] + ra1[1].astype(f32) + ra2[...]
     )
-    new_first[:, 0:half] = nf_a
-    new_second[:, 0:half] = ns_a
+    first[:, 0:half] = nf_a
+    second[:, 0:half] = ns_a
     updates[i, :, 0:half] = up_a
     got(rb2, h2_recv.at[1], h2_send.at[1])
     nf_b, ns_b, up_b = adam(
         first[:, half:rank], second[:, half:rank], grad[mine, :, half:rank] + rb1[1].astype(f32) + rb2[...]
     )
-    new_first[:, half:rank] = nf_b
-    new_second[:, half:rank] = ns_b
+    first[:, half:rank] = nf_b
+    second[:, half:rank] = ns_b
     updates[i, :, half:rank] = up_b
     stage1(updates, 0, 3)
 
-    basis_in(2)
-    stage2(rows_out, shard_of(1) * ndp, 1)
-    stage3(rows_out, shard_of(0) * ndp, 0)
+    store_first = pltpu.make_async_copy(first, first_out, store_sem.at[4])
+    store_second = pltpu.make_async_copy(second, second_out, store_sem.at[5])
+    store_first.start()
+    store_second.start()
+
+    stage3(rows, shard_of(2) * ndp, 2)
+    for g in range(3):
+        stage4(rows, shard_of(g) * ndp, g)
+        basis_sent(g)
+    loads[5].wait()
+
+    chunk = 4
+    pair_rows = 2 * own_rows
+    wide = chunk * own_rows
+
+    def decode(n, o):
+        pair = o // 2
+        got(block(updates, 0, o + 1 - 2 * core), pg_recv.at[3, 4 + n], pg_send.at[3, 4 + n])
+        left = updates[pl.ds(2 * pair, 2)].reshape(pair_rows, rank)
+        at = pl.ds(pl.multiple_of(pair * pair_rows, pair_rows), pair_rows)
+
+        def body(c, carry):
+            cols = pl.ds(pl.multiple_of(c * wide, wide), wide)
+            right = rows[pl.ds(c * chunk, chunk)].reshape(wide, rank)
+            decoded = times_basis(left, right)
+            weight[at, cols] = (weight[at, cols].astype(f32) - step_rate * decoded).astype(bf16)
+            return carry
+
+        lax.fori_loop(0, nf * ndp // chunk, body, 0)
+        pltpu.make_async_copy(weight.at[at], weight_out.at[at], store_sem.at[n]).start()
+
+    decode(0, i)
     stage2(updates, 0, 3)
-    stage3(rows_out, shard_of(1) * ndp, 1)
-    stage2(rows_out, shard_of(2) * ndp, 2)
+    decode(1, xn)
     stage3(updates, 0, 3)
-    stage3(rows_out, shard_of(2) * ndp, 2)
-    for g in range(3):
-        stage4(rows_out, shard_of(g) * ndp, g)
-        basis_sent(g)
-    stage4(updates, 0, 3)
-
-    own_copy.wait()
+    decode(2, yn)
+    decode(3, dn)
+    stage4(updates, 0, 3, False)
 
     @pl.when(j < nf - 1)
     def _():
-        sent(basis.at[i], z_send.at[0], z_recv.at[j])
+        sent(basis_in_ref.at[i], z_send.at[0], z_recv.at[j])
 
     @pl.when(j > 0)
     def _():
-        sent(basis.at[i], z_send.at[1], z_recv.at[j])
+        sent(basis_in_ref.at[i], z_send.at[1], z_recv.at[j])
 
     for d in (1, 2, 3):
         z = (j + d) % nf
@@ -269,6 +316,11 @@
         sent(sb1.at[n], h1_send.at[2 + n], h1_recv.at[2 + n])
     sent(sa2, h2_send.at[0], h2_recv.at[0])
     sent(sb2, h2_send.at[1], h2_recv.at[1])
+    store_first.wait()
+    store_second.wait()
+    for n, o in enumerate((i, xn, yn, dn)):
+        at = pl.ds(pl.multiple_of(o // 2 * pair_rows, pair_rows), pair_rows)
+        pltpu.make_async_copy(weight.at[at], weight_out.at[at], store_sem.at[n]).wait()
 
 
 def local_fused(activations, output_grads, basis, weight, first_moment, second_moment):
@@ -277,19 +329,25 @@
     own_rows = first_moment.shape[0]
     ndp, nf = lax.axis_size("dp"), lax.axis_size("fsdp")
     half = rank // 2
-    vmem = pl.BlockSpec(memory_space=pltpu.VMEM)
+    anywhere = pl.BlockSpec(memory_space=pl.ANY)
     dma = pltpu.SemaphoreType.DMA
-    updates, rows, new_first, new_second = pl.pallas_call(
-        exchange_kernel,
+    return pl.pallas_call(
+        fused_kernel,
         out_shape=(
-            jax.ShapeDtypeStruct((ndp, own_rows, rank), bf16),
-            jax.ShapeDtypeStruct((nf * ndp, own_rows, rank), bf16),
+            jax.ShapeDtypeStruct(weight.shape, bf16),
             jax.ShapeDtypeStruct((own_rows, rank), f32),
             jax.ShapeDtypeStruct((own_rows, rank), f32),
         ),
-        in_specs=[vmem] * 5,
-        out_specs=(vmem, pl.BlockSpec(memory_space=pl.ANY), vmem, vmem),
+        in_specs=[anywhere] * 6,
+        out_specs=(anywhere,) * 3,
         scratch_shapes=[
+            pltpu.VMEM(activations.shape, bf16),
+            pltpu.VMEM(output_grads.shape, bf16),
+            pltpu.VMEM((nf * ndp, own_rows, rank), bf16),
+            pltpu.VMEM(weight.shape, bf16),
+            pltpu.VMEM((own_rows, rank), f32),
+            pltpu.VMEM((own_rows, rank), f32),
+            pltpu.VMEM((ndp, own_rows, rank), bf16),
             pltpu.VMEM((nf, tokens // nf, rank), f32),
             pltpu.VMEM((nf, tokens // nf, rank), bf16),
             pltpu.VMEM((nf, tokens // nf, rank), bf16),
@@ -304,21 +362,19 @@
             pltpu.VMEM((own_rows, half), f32),
             pltpu.VMEM((own_rows, half), f32),
             pltpu.VMEM((own_rows, half), f32),
-            dma, dma((2,)), dma((3,)), dma((nf,)), dma((nf,)), dma((nf,)), dma((nf,)), dma((nf,)),
+            dma((6,)), dma((6,)), dma((2,)), dma((3,)), dma((nf,)), dma((nf,)), dma((nf,)), dma((nf,)), dma((nf,)),
             dma((4,)), dma((4,)), dma((4,)), dma((4,)), dma((2,)), dma((2,)), dma((4, 8)), dma((4, 8)),
         ],
         compiler_params=pltpu.CompilerParams(
-            collective_id=0, has_side_effects=True, vmem_limit_bytes=48 * 1024 * 1024
+            collective_id=0, has_side_effects=True, vmem_limit_bytes=63 * 1024 * 1024
         ),
         cost_estimate=pl.CostEstimate(
-            flops=4 * tokens * shard_rows * rank, bytes_accessed=24 * 1024 * 1024, transcendentals=0
+            flops=2 * shard_rows * rank * (2 * tokens + nf * shard_rows), bytes_accessed=24 * 1024 * 1024, transcendentals=0
         ),
     )(
-        activations, output_grads, basis.reshape(ndp, own_rows, rank), first_moment, second_moment
+        activations, output_grads, basis.reshape(ndp, own_rows, rank), weight,
+        first_moment, second_moment,
     )
-    decoded = times_basis(updates.reshape(shard_rows, rank), rows.reshape(nf * shard_rows, rank))
-    new_weight = (weight.astype(f32) - step_rate * decoded).astype(bf16)
-    return (new_weight, new_first, new_second)
 
 
 def local(activations, output_grads, basis, weight, first_moment, second_moment):

time: 108 us -> 101 us (0.935)
  matrix products: 15.2 us -> 0 us
  Pallas kernels: 85.6 us -> 90.5 us
  local copies, waits for them, and re-layouts: 5.74 us -> 9.57 us
    dot_general x1 -> x0, matrix products: 15.2 us -> none  [times_basis(): lax.dot_general(update, rows, (((1,), (1,)), ((), ())), preferred_element...]
    pallas_call x1, Pallas kernels: 85.6 us -> 90.5 us  [local_fused(): pl.pallas_call(fused_kernel, out_shape=(jax.ShapeDtypeStruct(weight.shape...]
    unnamed x10 -> x7, local copies, waits for them, and re-layouts: 5.74 us -> 9.57 us
where the time goes in v2:
time: 101 us
  Pallas kernels  90.5 us (90%)
  local copies, waits for them, and re-layouts  9.57 us (9%)
    pallas_call x1, Pallas kernels, local_fused(): pl.pallas_call(fused_kernel, out_shape=(jax.ShapeDtypeStruct(weight.shape...  90.5 us
    unnamed x7, local copies, waits for them, and re-layouts  9.57 us

profile of v2, /device:TPU:0, one launch (start us, length us, event | category | flops | bytes accessed | tf_op | source)
XLA Modules:
  0.0 100.7 jit_solution(9326393329032460581)
XLA Ops:
  0.6 90.5 %shard_map.85 = (bf16[1024,4096]{1,0:T(8,128)(2,1)}, f32[128,1024]{1,0:T(8,128)}, f32[128,1024]{1,0:T(8,128)}) custom-call(bf16[256,1024]{1,0:T(8,128)(2,1)} %act_in.1, bf16[256,1024]{1,0:T(8,128)(2,1)} %og_in.1, bf16[8,128,1024]{2,1,0:T(8,128)(2,1)} %bitcast.1, bf16[1024,4096]{1,0:T(8,128)(2,1)} %weight_in.1, f32[128,1024]{1,0:T(8,128)} %first_in.1, ...), custom_call_target="tpu_custom_call" | custom-call | flops 9663676416 | bytes 25165824 | tf_op jit(solution)/shard_map/pallas_call | solution.py:334
  91.1 0.0 copy-start.1
  91.1 0.0 copy-start
  91.2 8.0 %copy.12 = bf16[1024,4096]{1,0:T(8,128)(2,1)} copy(bf16[1024,4096]{1,0:T(8,128)(2,1)} %get-tuple-element.6) | data formatting | bytes 16777216
  99.1 0.0 copy-done.1
  99.1 0.8 copy.13
  99.9 0.0 copy-done
  99.9 0.8 copy.14
Async XLA Ops:
  91.1 8.0 %copy-start.1 = (f32[128,1024]{1,0:T(8,128)S(1)}, f32[128,1024]{1,0:T(8,128)}, u32[]{:S(2)}) copy-start(f32[128,1024]{1,0:T(8,128)} %get-tuple-element.7) | copy-start | bytes 1572868
  91.1 8.8 %copy-start = (f32[128,1024]{1,0:T(8,128)S(1)}, f32[128,1024]{1,0:T(8,128)}, u32[]{:S(2)}) copy-start(f32[128,1024]{1,0:T(8,128)} %get-tuple-element.8) | copy-start | bytes 1572868

commit v3 on v2

--- a/solution.py
+++ b/solution.py
@@ -182,6 +182,7 @@
             sent(z_piece(s), z_fwd.at[g], z_recv.at[s])
 
     basis_in(0)
+    basis_in(1)
 
     total = part[j]
     for d in (1, 2, 3):
@@ -194,7 +195,7 @@
         remote(proj.at[j], proj.at[j], ag_send.at[z], ag_recv.at[j], i, z).start()
 
     stage2(rows, shard_of(0) * ndp, 0)
-    basis_in(1)
+    basis_in(2)
     stage3(rows, shard_of(0) * ndp, 0)
     stage2(rows, shard_of(1) * ndp, 1)
 
@@ -211,47 +212,57 @@
             og[:, cols], projected, (((0,), (0,)), ((), ())), preferred_element_type=f32
         ) / total_tokens
 
+    mine = 2 * y + x
+    order = (3 - mine, 2 * y + 1 - x, 2 * (1 - y) + x, mine)
     for q in range(4):
-        grad[4 + q] = term(2 * q + 1 - core)
+        grad[4 + q] = term(2 * order[q] + 1 - core)
         remote(grad.at[4 + q], grad_core.at[q], core_send.at[q], core_recv.at[q], sib, j).start()
-    basis_in(2)
     for q in range(4):
-        grad[q] = term(2 * q + core)
-    for q in range(4):
+        grad[q] = term(2 * order[q] + core)
+
+    def pair_sum(q):
         got(grad_core.at[q], core_recv.at[q], core_send.at[q])
         grad[q] = grad[q] + grad_core[q]
 
-    for n, far in enumerate((1, 0)):
-        yy = far * (1 - y) + (1 - far) * y
-        sa1[n] = grad[2 * yy + 1 - x, :, 0:half].astype(bf16)
-        remote(sa1.at[n], ra1.at[n], h1_send.at[n], h1_recv.at[n], xn, j).start()
-        xx = far * (1 - x) + (1 - far) * x
-        sb1[n] = grad[2 * (1 - y) + xx, :, half:rank].astype(bf16)
-        remote(sb1.at[n], rb1.at[n], h1_send.at[2 + n], h1_recv.at[2 + n], yn, j).start()
+    def hop1(n, qa, qb):
+        if qa is not None:
+            sa1[n] = grad[qa, :, 0:half].astype(bf16)
+            remote(sa1.at[n], ra1.at[n], h1_send.at[n], h1_recv.at[n], xn, j).start()
+        if qb is not None:
+            sb1[n] = grad[qb, :, half:rank].astype(bf16)
+            remote(sb1.at[n], rb1.at[n], h1_send.at[2 + n], h1_recv.at[2 + n], yn, j).start()
+
+    pair_sum(0)
+    hop1(0, 0, 0)
+    pair_sum(1)
+    hop1(1, 1, None)
+    pair_sum(2)
+    hop1(1, None, 2)
+    pair_sum(3)
     stage3(rows, shard_of(1) * ndp, 1)
+    stage2(rows, shard_of(2) * ndp, 2)
     got(ra1.at[0], h1_recv.at[0], h1_send.at[0])
-    sa2[...] = grad[2 * (1 - y) + x, :, 0:half] + ra1[0].astype(f32)
+    sa2[...] = grad[2, :, 0:half] + ra1[0].astype(f32)
     remote(sa2, ra2, h2_send.at[0], h2_recv.at[0], yn, j).start()
     got(rb1.at[0], h1_recv.at[2], h1_send.at[2])
-    sb2[...] = grad[2 * y + 1 - x, :, half:rank] + rb1[0].astype(f32)
+    sb2[...] = grad[1, :, half:rank] + rb1[0].astype(f32)
     remote(sb2, rb2, h2_send.at[1], h2_recv.at[1], xn, j).start()
     got(ra1.at[1], h1_recv.at[1], h1_send.at[1])
     got(rb1.at[1], h1_recv.at[3], h1_send.at[3])
 
-    stage2(rows, shard_of(2) * ndp, 2)
-    mine = 2 * y + x
+    stage3(rows, shard_of(2) * ndp, 2)
     loads[3].wait()
     loads[4].wait()
     got(ra2, h2_recv.at[0], h2_send.at[0])
     nf_a, ns_a, up_a = adam(
-        first[:, 0:half], second[:, 0:half], grad[mine, :, 0:half] + ra1[1].astype(f32) + ra2[...]
+        first[:, 0:half], second[:, 0:half], grad[3, :, 0:half] + ra1[1].astype(f32) + ra2[...]
     )
     first[:, 0:half] = nf_a
     second[:, 0:half] = ns_a
     updates[i, :, 0:half] = up_a
     got(rb2, h2_recv.at[1], h2_send.at[1])
     nf_b, ns_b, up_b = adam(
-        first[:, half:rank], second[:, half:rank], grad[mine, :, half:rank] + rb1[1].astype(f32) + rb2[...]
+        first[:, half:rank], second[:, half:rank], grad[3, :, half:rank] + rb1[1].astype(f32) + rb2[...]
     )
     first[:, half:rank] = nf_b
     second[:, half:rank] = ns_b
@@ -263,7 +274,6 @@
     store_first.start()
     store_second.start()
 
-    stage3(rows, shard_of(2) * ndp, 2)
     for g in range(3):
         stage4(rows, shard_of(g) * ndp, g)
         basis_sent(g)
@@ -323,6 +333,22 @@
         pltpu.make_async_copy(weight.at[at], weight_out.at[at], store_sem.at[n]).wait()
 
 
+def store_kernel(*refs):
+    n = len(refs) // 2
+    sources, targets, sem = refs[:n], refs[n : 2 * n], refs[2 * n]
+    copies = []
+    for source, target in zip(sources, targets):
+        pieces = 8 if source.dtype == bf16 else 1
+        size = source.shape[0] // pieces
+        for k in range(pieces):
+            at = pl.ds(k * size, size)
+            copies.append(pltpu.make_async_copy(source.at[at], target.at[at], sem.at[len(copies)]))
+    for copy in copies:
+        copy.start()
+    for copy in copies:
+        copy.wait()
+
+
 def local_fused(activations, output_grads, basis, weight, first_moment, second_moment):
     tokens, _ = activations.shape
     shard_rows, rank = basis.shape
@@ -331,7 +357,7 @@
     half = rank // 2
     anywhere = pl.BlockSpec(memory_space=pl.ANY)
     dma = pltpu.SemaphoreType.DMA
-    return pl.pallas_call(
+    results = pl.pallas_call(
         fused_kernel,
         out_shape=(
             jax.ShapeDtypeStruct(weight.shape, bf16),
@@ -375,6 +401,14 @@
         activations, output_grads, basis.reshape(ndp, own_rows, rank), weight,
         first_moment, second_moment,
     )
+    return pl.pallas_call(
+        store_kernel,
+        out_shape=[jax.ShapeDtypeStruct(r.shape, r.dtype) for r in results],
+        in_specs=[anywhere] * 3,
+        out_specs=[anywhere] * 3,
+        scratch_shapes=[dma((10,))],
+        compiler_params=pltpu.CompilerParams(vmem_limit_bytes=63 * 1024 * 1024),
+    )(*results)
 
 
 def local(activations, output_grads, basis, weight, first_moment, second_moment):

time: 101 us -> 372 us (3.68)
  Pallas kernels: 90.5 us -> 370 us
  local copies, waits for them, and re-layouts: 9.57 us -> 0 us
    pallas_call x0 -> x1, Pallas kernels: none -> 287 us  [local_fused(): pl.pallas_call(store_kernel, out_shape=[jax.ShapeDtypeStruct(r.shape, r.d...]
    unnamed x7 -> x0, local copies, waits for them, and re-layouts: 9.57 us -> none
    pallas_call x1, Pallas kernels: 90.5 us -> 83.4 us  [local_fused(): pl.pallas_call(fused_kernel, out_shape=(jax.ShapeDtypeStruct(weight.shape...]
where the time goes in v3:
time: 372 us; the launch traced here: 371 us
  Pallas kernels  370 us (99%)
    pallas_call x1, Pallas kernels, local_fused(): pl.pallas_call(store_kernel, out_shape=[jax.ShapeDtypeStruct(r.shape, r.d...  287 us
    pallas_call x1, Pallas kernels, local_fused(): pl.pallas_call(fused_kernel, out_shape=(jax.ShapeDtypeStruct(weight.shape...  83.4 us

profile of v3, /device:TPU:0, one launch (start us, length us, event | category | flops | bytes accessed | tf_op | source)
XLA Modules:
  0.0 371.1 jit_solution(15506360659456080280)
XLA Ops:
  0.6 83.4 %shard_map.85 = (bf16[1024,4096]{1,0:T(8,128)(2,1)}, f32[128,1024]{1,0:T(8,128)}, f32[128,1024]{1,0:T(8,128)}) custom-call(bf16[256,1024]{1,0:T(8,128)(2,1)} %act_in.1, bf16[256,1024]{1,0:T(8,128)(2,1)} %og_in.1, bf16[8,128,1024]{2,1,0:T(8,128)(2,1)} %bitcast.1, bf16[1024,4096]{1,0:T(8,128)(2,1)} %weight_in.1, f32[128,1024]{1,0:T(8,128)} %first_in.1, ...), custom_call_target="tpu_custom_call" | custom-call | flops 9663676416 | bytes 25165824 | tf_op jit(solution)/shard_map/pallas_call | solution.py:360
  84.1 287.1 %shard_map.86 = (bf16[1024,4096]{1,0:T(8,128)(2,1)}, f32[128,1024]{1,0:T(8,128)}, f32[128,1024]{1,0:T(8,128)}) custom-call(bf16[1024,4096]{1,0:T(8,128)(2,1)} %get-tuple-element.6.refs_0_, f32[128,1024]{1,0:T(8,128)} %get-tuple-element.7.refs_1_, f32[128,1024]{1,0:T(8,128)} %get-tuple-element.8.refs_2_), custom_call_target="tpu_custom_call" | custom-call | tf_op jit(solution)/shard_map/pallas_call | solution.py:404

commit v4 on v3

--- a/solution.py
+++ b/solution.py
@@ -98,11 +98,11 @@
 
     loads[0].wait()
     loads[1].wait()
-    a = act[...]
-    acc = None
-    for k in range(ndp):
-        term = jnp.dot(a[:, k * own_rows : (k + 1) * own_rows], rows[j * ndp + k], preferred_element_type=f32)
-        acc = term if acc is None else acc + term
+    acc = jnp.dot(
+        act[...],
+        rows[pl.ds(j * ndp, ndp)].reshape(ndp * own_rows, rank),
+        preferred_element_type=f32,
+    )
     part[...] = acc.reshape(nf, tb, rank)
     part_send[...] = acc.reshape(nf, tb, rank).astype(bf16)
     for d in (1, 2, 3):
@@ -210,7 +210,7 @@
         cols = pl.ds(pl.multiple_of(k * own_rows, own_rows), own_rows)
         return lax.dot_general(
             og[:, cols], projected, (((0,), (0,)), ((), ())), preferred_element_type=f32
-        ) / total_tokens
+        )
 
     mine = 2 * y + x
     order = (3 - mine, 2 * y + 1 - x, 2 * (1 - y) + x, mine)
@@ -255,14 +255,14 @@
     loads[4].wait()
     got(ra2, h2_recv.at[0], h2_send.at[0])
     nf_a, ns_a, up_a = adam(
-        first[:, 0:half], second[:, 0:half], grad[3, :, 0:half] + ra1[1].astype(f32) + ra2[...]
+        first[:, 0:half], second[:, 0:half], (grad[3, :, 0:half] + ra1[1].astype(f32) + ra2[...]) / total_tokens
     )
     first[:, 0:half] = nf_a
     second[:, 0:half] = ns_a
     updates[i, :, 0:half] = up_a
     got(rb2, h2_recv.at[1], h2_send.at[1])
     nf_b, ns_b, up_b = adam(
-        first[:, half:rank], second[:, half:rank], grad[3, :, half:rank] + rb1[1].astype(f32) + rb2[...]
+        first[:, half:rank], second[:, half:rank], (grad[3, :, half:rank] + rb1[1].astype(f32) + rb2[...]) / total_tokens
     )
     first[:, half:rank] = nf_b
     second[:, half:rank] = ns_b
@@ -333,19 +333,25 @@
         pltpu.make_async_copy(weight.at[at], weight_out.at[at], store_sem.at[n]).wait()
 
 
-def store_kernel(*refs):
-    n = len(refs) // 2
-    sources, targets, sem = refs[:n], refs[n : 2 * n], refs[2 * n]
-    copies = []
-    for source, target in zip(sources, targets):
-        pieces = 8 if source.dtype == bf16 else 1
-        size = source.shape[0] // pieces
-        for k in range(pieces):
-            at = pl.ds(k * size, size)
-            copies.append(pltpu.make_async_copy(source.at[at], target.at[at], sem.at[len(copies)]))
-    for copy in copies:
+def store_kernel(
+    weight, first, second, weight_out, first_out, second_out,
+    weight_buf, first_buf, second_buf, in_sem, out_sem,
+):
+    pieces = 16
+    size = weight.shape[0] // pieces
+    parts = [
+        (weight.at[pl.ds(k * size, size)], weight_buf.at[pl.ds(k * size, size)],
+         weight_out.at[pl.ds(k * size, size)])
+        for k in range(pieces)
+    ] + [(first, first_buf, first_out), (second, second_buf, second_out)]
+    ins = [pltpu.make_async_copy(a, b, in_sem.at[n]) for n, (a, b, _) in enumerate(parts)]
+    outs = [pltpu.make_async_copy(b, c, out_sem.at[n]) for n, (_, b, c) in enumerate(parts)]
+    for copy in ins:
         copy.start()
-    for copy in copies:
+    for load, store in zip(ins, outs):
+        load.wait()
+        store.start()
+    for copy in outs:
         copy.wait()
 
 
@@ -406,7 +412,7 @@
         out_shape=[jax.ShapeDtypeStruct(r.shape, r.dtype) for r in results],
         in_specs=[anywhere] * 3,
         out_specs=[anywhere] * 3,
-        scratch_shapes=[dma((10,))],
+        scratch_shapes=[pltpu.VMEM(r.shape, r.dtype) for r in results] + [dma((18,)), dma((18,))],
         compiler_params=pltpu.CompilerParams(vmem_limit_bytes=63 * 1024 * 1024),
     )(*results)
 

time: 372 us -> 92.7 us (0.25)
  Pallas kernels: 370 us -> 91 us
    pallas_call x1, Pallas kernels: 287 us -> 7.52 us  [local_fused(): pl.pallas_call(store_kernel, out_shape=[jax.ShapeDtypeStruct(r.shape, r.d...]
where the time goes in v4:
time: 92.7 us; the launch traced here: 91.6 us
  Pallas kernels  91 us (98%)
    pallas_call x1, Pallas kernels, local_fused(): pl.pallas_call(fused_kernel, out_shape=(jax.ShapeDtypeStruct(weight.shape...  83.5 us
    pallas_call x1, Pallas kernels, local_fused(): pl.pallas_call(store_kernel, out_shape=[jax.ShapeDtypeStruct(r.shape, r.d...  7.52 us

profile of v4, /device:TPU:0, one launch (start us, length us, event | category | flops | bytes accessed | tf_op | source)
XLA Modules:
  0.0 91.6 jit_solution(13066266407986941205)
XLA Ops:
  0.6 83.5 %shard_map.85 = (bf16[1024,4096]{1,0:T(8,128)(2,1)}, f32[128,1024]{1,0:T(8,128)}, f32[128,1024]{1,0:T(8,128)}) custom-call(bf16[256,1024]{1,0:T(8,128)(2,1)} %act_in.1, bf16[256,1024]{1,0:T(8,128)(2,1)} %og_in.1, bf16[8,128,1024]{2,1,0:T(8,128)(2,1)} %bitcast.1, bf16[1024,4096]{1,0:T(8,128)(2,1)} %weight_in.1, f32[128,1024]{1,0:T(8,128)} %first_in.1, ...), custom_call_target="tpu_custom_call" | custom-call | flops 9663676416 | bytes 25165824 | tf_op jit(solution)/shard_map/pallas_call | solution.py:366
  84.1 7.5 %shard_map.86 = (bf16[1024,4096]{1,0:T(8,128)(2,1)}, f32[128,1024]{1,0:T(8,128)}, f32[128,1024]{1,0:T(8,128)}) custom-call(bf16[1024,4096]{1,0:T(8,128)(2,1)} %get-tuple-element.6.weight, f32[128,1024]{1,0:T(8,128)} %get-tuple-element.7.first, f32[128,1024]{1,0:T(8,128)} %get-tuple-element.8.second), custom_call_target="tpu_custom_call" | custom-call | tf_op jit(solution)/shard_map/pallas_call | solution.py:410

commit v5 on v4

--- a/solution.py
+++ b/solution.py
@@ -49,8 +49,10 @@
     tokens, rank = act.shape[0], first.shape[1]
     own_rows = first.shape[0]
     tb = tokens // nf
-    half = rank // 2
     total_tokens = tokens * ndp
+    chunks = part.shape[0]
+    width = rank // chunks
+    lane = width // 2
 
     loads = [
         pltpu.make_async_copy(src, dst, load_sem.at[n])
@@ -98,60 +100,85 @@
 
     loads[0].wait()
     loads[1].wait()
-    acc = jnp.dot(
-        act[...],
-        rows[pl.ds(j * ndp, ndp)].reshape(ndp * own_rows, rank),
-        preferred_element_type=f32,
-    )
-    part[...] = acc.reshape(nf, tb, rank)
-    part_send[...] = acc.reshape(nf, tb, rank).astype(bf16)
-    for d in (1, 2, 3):
-        z = (j + d) % nf
-        remote(part_send.at[z], part_recv.at[j], rs_send.at[z], rs_recv.at[j], i, z).start()
-
-    def block(buf, base, k):
-        return buf.at[base + k]
-
-    def lane_a(buf, base, k):
-        return buf.at[base + k, :, pl.ds(0, half)]
-
-    def lane_b(buf, base, k):
-        return buf.at[base + k, :, pl.ds(half, half)]
-
-    def stage1(buf, base, g):
-        mine = block(buf, base, i)
+
+    def partial(c):
+        acc = jnp.dot(
+            act[...],
+            rows[pl.ds(j * ndp, ndp), :, c * width : (c + 1) * width].reshape(ndp * own_rows, width),
+            preferred_element_type=f32,
+        ).reshape(nf, tb, width)
+        part[c] = acc
+        part_send[c] = acc.astype(bf16)
+
+    def scatter(c):
+        for d in (2, 1, 3):
+            z = (j + d) % nf
+            remote(part_send.at[c, z], part_recv.at[c, j], rs_send.at[c, z], rs_recv.at[c, j], i, z).start()
+
+    def reduce_gather(c):
+        total = part[c, j]
+        for d in (1, 2, 3):
+            z = (j + d) % nf
+            got(part_recv.at[c, z], rs_recv.at[c, z], rs_send.at[c, z])
+            total = total + part_recv[c, z].astype(f32)
+        proj[c, j] = total.astype(bf16)
+        for d in (2, 1, 3):
+            z = (j + d) % nf
+            remote(proj.at[c, j], proj.at[c, j], ag_send.at[c, z], ag_recv.at[c, j], i, z).start()
+
+    partial(0)
+    scatter(0)
+    for c in range(1, chunks):
+        partial(c)
+
+    def columns(g, base, k, start, stop):
+        if g < 3:
+            return rows.at[base + k, :, pl.ds(rank * start // 2, rank * (stop - start) // 2)]
+        return updates.at[k, :, pl.ds((g - 3) * width + lane * start, lane * (stop - start))]
+
+    def block(g, base, k):
+        return columns(g, base, k, 0, 2)
+
+    def lane_a(g, base, k):
+        return columns(g, base, k, 0, 1)
+
+    def lane_b(g, base, k):
+        return columns(g, base, k, 1, 2)
+
+    def stage1(base, g):
+        mine = block(g, base, i)
         remote(mine, mine, pg_send.at[g, 0], pg_recv.at[g, 0], xn, j).start()
         remote(mine, mine, pg_send.at[g, 1], pg_recv.at[g, 1], yn, j).start()
         remote(mine, mine, pg_send.at[g, 4], pg_recv.at[g, 4], sib, j).start()
 
-    def stage2(buf, base, g):
-        bx, by = block(buf, base, xn), block(buf, base, yn)
+    def stage2(base, g):
+        bx, by = block(g, base, xn), block(g, base, yn)
         got(bx, pg_recv.at[g, 0], pg_send.at[g, 0])
-        lb = lane_b(buf, base, xn)
+        lb = lane_b(g, base, xn)
         remote(lb, lb, pg_send.at[g, 3], pg_recv.at[g, 3], yn, j).start()
         remote(bx, bx, pg_send.at[g, 5], pg_recv.at[g, 5], sib, j).start()
         got(by, pg_recv.at[g, 1], pg_send.at[g, 1])
-        la = lane_a(buf, base, yn)
+        la = lane_a(g, base, yn)
         remote(la, la, pg_send.at[g, 2], pg_recv.at[g, 2], xn, j).start()
         remote(by, by, pg_send.at[g, 6], pg_recv.at[g, 6], sib, j).start()
 
-    def stage3(buf, base, g):
-        got(lane_a(buf, base, dn), pg_recv.at[g, 2], pg_send.at[g, 2])
-        got(lane_b(buf, base, dn), pg_recv.at[g, 3], pg_send.at[g, 3])
-        bd = block(buf, base, dn)
+    def stage3(base, g):
+        got(lane_a(g, base, dn), pg_recv.at[g, 2], pg_send.at[g, 2])
+        got(lane_b(g, base, dn), pg_recv.at[g, 3], pg_send.at[g, 3])
+        bd = block(g, base, dn)
         remote(bd, bd, pg_send.at[g, 7], pg_recv.at[g, 7], sib, j).start()
 
-    def stage4(buf, base, g, receive=True):
+    def stage4(base, g, receive=True):
         for q in range(4):
             o = (i, xn, yn, dn)[q]
             so = o + 1 - 2 * core
             if receive:
-                got(block(buf, base, so), pg_recv.at[g, 4 + q], pg_send.at[g, 4 + q])
-            sent(block(buf, base, o), pg_send.at[g, 4 + q], pg_recv.at[g, 4 + q])
-        sent(block(buf, base, i), pg_send.at[g, 0], pg_recv.at[g, 0])
-        sent(block(buf, base, i), pg_send.at[g, 1], pg_recv.at[g, 1])
-        sent(lane_a(buf, base, yn), pg_send.at[g, 2], pg_recv.at[g, 2])
-        sent(lane_b(buf, base, xn), pg_send.at[g, 3], pg_recv.at[g, 3])
+                got(block(g, base, so), pg_recv.at[g, 4 + q], pg_send.at[g, 4 + q])
+            sent(block(g, base, o), pg_send.at[g, 4 + q], pg_recv.at[g, 4 + q])
+        sent(block(g, base, i), pg_send.at[g, 0], pg_recv.at[g, 0])
+        sent(block(g, base, i), pg_send.at[g, 1], pg_recv.at[g, 1])
+        sent(lane_a(g, base, yn), pg_send.at[g, 2], pg_recv.at[g, 2])
+        sent(lane_b(g, base, xn), pg_send.at[g, 3], pg_recv.at[g, 3])
 
     low = 1 - j // 2
     edge = low * j + (1 - low) * (nf - 1 - j)
@@ -172,7 +199,7 @@
         def _():
             remote(z_piece(s), z_piece(s), z_fwd.at[g], z_recv.at[s], i, j - 1).start()
 
-        stage1(rows, s * ndp, g)
+        stage1(s * ndp, g)
 
     def basis_sent(g):
         s = shard_of(g)
@@ -181,101 +208,104 @@
         def _():
             sent(z_piece(s), z_fwd.at[g], z_recv.at[s])
 
-    basis_in(0)
-    basis_in(1)
-
-    total = part[j]
-    for d in (1, 2, 3):
-        z = (j + d) % nf
-        got(part_recv.at[z], rs_recv.at[z], rs_send.at[z])
-        total = total + part_recv[z].astype(f32)
-    proj[j] = total.astype(bf16)
-    for d in (1, 2, 3):
-        z = (j + d) % nf
-        remote(proj.at[j], proj.at[j], ag_send.at[z], ag_recv.at[j], i, z).start()
-
-    stage2(rows, shard_of(0) * ndp, 0)
-    basis_in(2)
-    stage3(rows, shard_of(0) * ndp, 0)
-    stage2(rows, shard_of(1) * ndp, 1)
-
-    for d in (1, 2, 3):
-        z = (j + d) % nf
-        got(proj.at[z], ag_recv.at[z], ag_send.at[z])
-
-    loads[2].wait()
-    projected = proj[...].reshape(tokens, rank)
-
-    def term(k):
-        cols = pl.ds(pl.multiple_of(k * own_rows, own_rows), own_rows)
-        return lax.dot_general(
-            og[:, cols], projected, (((0,), (0,)), ((), ())), preferred_element_type=f32
-        )
-
     mine = 2 * y + x
     order = (3 - mine, 2 * y + 1 - x, 2 * (1 - y) + x, mine)
-    for q in range(4):
-        grad[4 + q] = term(2 * order[q] + 1 - core)
-        remote(grad.at[4 + q], grad_core.at[q], core_send.at[q], core_recv.at[q], sib, j).start()
-    for q in range(4):
-        grad[q] = term(2 * order[q] + core)
-
-    def pair_sum(q):
-        got(grad_core.at[q], core_recv.at[q], core_send.at[q])
-        grad[q] = grad[q] + grad_core[q]
-
-    def hop1(n, qa, qb):
-        if qa is not None:
-            sa1[n] = grad[qa, :, 0:half].astype(bf16)
-            remote(sa1.at[n], ra1.at[n], h1_send.at[n], h1_recv.at[n], xn, j).start()
-        if qb is not None:
-            sb1[n] = grad[qb, :, half:rank].astype(bf16)
-            remote(sb1.at[n], rb1.at[n], h1_send.at[2 + n], h1_recv.at[2 + n], yn, j).start()
-
-    pair_sum(0)
-    hop1(0, 0, 0)
-    pair_sum(1)
-    hop1(1, 1, None)
-    pair_sum(2)
-    hop1(1, None, 2)
-    pair_sum(3)
-    stage3(rows, shard_of(1) * ndp, 1)
-    stage2(rows, shard_of(2) * ndp, 2)
-    got(ra1.at[0], h1_recv.at[0], h1_send.at[0])
-    sa2[...] = grad[2, :, 0:half] + ra1[0].astype(f32)
-    remote(sa2, ra2, h2_send.at[0], h2_recv.at[0], yn, j).start()
-    got(rb1.at[0], h1_recv.at[2], h1_send.at[2])
-    sb2[...] = grad[1, :, half:rank] + rb1[0].astype(f32)
-    remote(sb2, rb2, h2_send.at[1], h2_recv.at[1], xn, j).start()
-    got(ra1.at[1], h1_recv.at[1], h1_send.at[1])
-    got(rb1.at[1], h1_recv.at[3], h1_send.at[3])
-
-    stage3(rows, shard_of(2) * ndp, 2)
+
+    def low_grad(c):
+        for d in (1, 2, 3):
+            z = (j + d) % nf
+            got(proj.at[c, z], ag_recv.at[c, z], ag_send.at[c, z])
+        projected = proj[c].reshape(tokens, width)
+
+        def term(k):
+            cols = pl.ds(pl.multiple_of(k * own_rows, own_rows), own_rows)
+            return lax.dot_general(
+                og[:, cols], projected, (((0,), (0,)), ((), ())), preferred_element_type=f32
+            )
+
+        for q in range(4):
+            grad[c, 4 + q] = term(2 * order[q] + 1 - core)
+            remote(
+                grad.at[c, 4 + q], grad_core.at[c, q], core_send.at[c, q], core_recv.at[c, q], sib, j
+            ).start()
+        for q in range(4):
+            grad[c, q] = term(2 * order[q] + core)
+
+    def hop1(c):
+        for q in range(4):
+            got(grad_core.at[c, q], core_recv.at[c, q], core_send.at[c, q])
+            grad[c, q] = grad[c, q] + grad_core[c, q]
+            if q in (0, 1):
+                sa1[c, q] = grad[c, q, :, 0:lane].astype(bf16)
+                remote(sa1.at[c, q], ra1.at[c, q], h1_send.at[c, q], h1_recv.at[c, q], xn, j).start()
+            if q in (0, 2):
+                n = q // 2
+                sb1[c, n] = grad[c, q, :, lane:width].astype(bf16)
+                remote(sb1.at[c, n], rb1.at[c, n], h1_send.at[c, 2 + n], h1_recv.at[c, 2 + n], yn, j).start()
+
+    def hop2(c):
+        got(ra1.at[c, 0], h1_recv.at[c, 0], h1_send.at[c, 0])
+        sa2[c] = grad[c, 2, :, 0:lane] + ra1[c, 0].astype(f32)
+        remote(sa2.at[c], ra2.at[c], h2_send.at[c, 0], h2_recv.at[c, 0], yn, j).start()
+        got(rb1.at[c, 0], h1_recv.at[c, 2], h1_send.at[c, 2])
+        sb2[c] = grad[c, 1, :, lane:width] + rb1[c, 0].astype(f32)
+        remote(sb2.at[c], rb2.at[c], h2_send.at[c, 1], h2_recv.at[c, 1], xn, j).start()
+
+    def step(c):
+        got(ra1.at[c, 1], h1_recv.at[c, 1], h1_send.at[c, 1])
+        got(rb1.at[c, 1], h1_recv.at[c, 3], h1_send.at[c, 3])
+        for n, (r1, r2) in enumerate(((ra1, ra2), (rb1, rb2))):
+            got(r2.at[c], h2_recv.at[c, n], h2_send.at[c, n])
+            cols = pl.ds(c * width + n * lane, lane)
+            summed = grad[c, 3, :, n * lane : (n + 1) * lane] + r1[c, 1].astype(f32) + r2[c]
+            first[:, cols], second[:, cols], updates[i, :, cols] = adam(
+                first[:, cols], second[:, cols], summed / total_tokens
+            )
+        stage1(0, 3 + c)
+
+    middle = (j > 0) & (j < nf - 1)
+    shard_base = [shard_of(g) * ndp for g in range(3)]
+    basis_in(0)
+    reduce_gather(0)
+    scatter(1)
+    basis_in(1)
+    stage2(shard_base[0], 0)
+
+    @pl.when(middle)
+    def _():
+        basis_in(2)
+
+    reduce_gather(1)
+    loads[2].wait()
+    low_grad(0)
+    hop1(0)
+    stage3(shard_base[0], 0)
+    stage2(shard_base[1], 1)
+    hop2(0)
+
+    @pl.when(jnp.logical_not(middle))
+    def _():
+        basis_in(2)
+
+    low_grad(1)
     loads[3].wait()
     loads[4].wait()
-    got(ra2, h2_recv.at[0], h2_send.at[0])
-    nf_a, ns_a, up_a = adam(
-        first[:, 0:half], second[:, 0:half], (grad[3, :, 0:half] + ra1[1].astype(f32) + ra2[...]) / total_tokens
-    )
-    first[:, 0:half] = nf_a
-    second[:, 0:half] = ns_a
-    updates[i, :, 0:half] = up_a
-    got(rb2, h2_recv.at[1], h2_send.at[1])
-    nf_b, ns_b, up_b = adam(
-        first[:, half:rank], second[:, half:rank], (grad[3, :, half:rank] + rb1[1].astype(f32) + rb2[...]) / total_tokens
-    )
-    first[:, half:rank] = nf_b
-    second[:, half:rank] = ns_b
-    updates[i, :, half:rank] = up_b
-    stage1(updates, 0, 3)
-
+    step(0)
+    hop1(1)
+    stage3(shard_base[1], 1)
+    stage2(shard_base[2], 2)
+    hop2(1)
+    stage2(0, 3)
+    stage3(shard_base[2], 2)
+    step(1)
+    stage3(0, 3)
     store_first = pltpu.make_async_copy(first, first_out, store_sem.at[4])
     store_second = pltpu.make_async_copy(second, second_out, store_sem.at[5])
     store_first.start()
     store_second.start()
 
     for g in range(3):
-        stage4(rows, shard_of(g) * ndp, g)
+        stage4(shard_base[g], g)
         basis_sent(g)
     loads[5].wait()
 
@@ -285,7 +315,8 @@
 
     def decode(n, o):
         pair = o // 2
-        got(block(updates, 0, o + 1 - 2 * core), pg_recv.at[3, 4 + n], pg_send.at[3, 4 + n])
+        for g in range(3, 3 + chunks):
+            got(block(g, 0, o + 1 - 2 * core), pg_recv.at[g, 4 + n], pg_send.at[g, 4 + n])
         left = updates[pl.ds(2 * pair, 2)].reshape(pair_rows, rank)
         at = pl.ds(pl.multiple_of(pair * pair_rows, pair_rows), pair_rows)
 
@@ -300,12 +331,13 @@
         pltpu.make_async_copy(weight.at[at], weight_out.at[at], store_sem.at[n]).start()
 
     decode(0, i)
-    stage2(updates, 0, 3)
+    stage2(0, 4)
     decode(1, xn)
-    stage3(updates, 0, 3)
+    stage3(0, 4)
     decode(2, yn)
     decode(3, dn)
-    stage4(updates, 0, 3, False)
+    stage4(0, 3, False)
+    stage4(0, 4, False)
 
     @pl.when(j < nf - 1)
     def _():
@@ -315,17 +347,18 @@
     def _():
         sent(basis_in_ref.at[i], z_send.at[1], z_recv.at[j])
 
-    for d in (1, 2, 3):
-        z = (j + d) % nf
-        sent(part_send.at[z], rs_send.at[z], rs_recv.at[z])
-        sent(proj.at[j], ag_send.at[z], ag_recv.at[z])
-    for q in range(4):
-        sent(grad.at[4 + q], core_send.at[q], core_recv.at[q])
-    for n in range(2):
-        sent(sa1.at[n], h1_send.at[n], h1_recv.at[n])
-        sent(sb1.at[n], h1_send.at[2 + n], h1_recv.at[2 + n])
-    sent(sa2, h2_send.at[0], h2_recv.at[0])
-    sent(sb2, h2_send.at[1], h2_recv.at[1])
+    for c in range(chunks):
+        for d in (1, 2, 3):
+            z = (j + d) % nf
+            sent(part_send.at[c, z], rs_send.at[c, z], rs_recv.at[c, z])
+            sent(proj.at[c, j], ag_send.at[c, z], ag_recv.at[c, z])
+        for q in range(4):
+            sent(grad.at[c, 4 + q], core_send.at[c, q], core_recv.at[c, q])
+        for n in range(2):
+            sent(sa1.at[c, n], h1_send.at[c, n], h1_recv.at[c, n])
+            sent(sb1.at[c, n], h1_send.at[c, 2 + n], h1_recv.at[c, 2 + n])
+        sent(sa2.at[c], h2_send.at[c, 0], h2_recv.at[c, 0])
+        sent(sb2.at[c], h2_send.at[c, 1], h2_recv.at[c, 1])
     store_first.wait()
     store_second.wait()
     for n, o in enumerate((i, xn, yn, dn)):
@@ -360,7 +393,8 @@
     shard_rows, rank = basis.shape
     own_rows = first_moment.shape[0]
     ndp, nf = lax.axis_size("dp"), lax.axis_size("fsdp")
-    half = rank // 2
+    chunks = 2
+    width = rank // chunks
     anywhere = pl.BlockSpec(memory_space=pl.ANY)
     dma = pltpu.SemaphoreType.DMA
     results = pl.pallas_call(
@@ -380,22 +414,14 @@
             pltpu.VMEM((own_rows, rank), f32),
             pltpu.VMEM((own_rows, rank), f32),
             pltpu.VMEM((ndp, own_rows, rank), bf16),
-            pltpu.VMEM((nf, tokens // nf, rank), f32),
-            pltpu.VMEM((nf, tokens // nf, rank), bf16),
-            pltpu.VMEM((nf, tokens // nf, rank), bf16),
-            pltpu.VMEM((nf, tokens // nf, rank), bf16),
-            pltpu.VMEM((ndp, own_rows, rank), f32),
-            pltpu.VMEM((ndp // 2, own_rows, rank), f32),
-            pltpu.VMEM((2, own_rows, half), bf16),
-            pltpu.VMEM((2, own_rows, half), bf16),
-            pltpu.VMEM((2, own_rows, half), bf16),
-            pltpu.VMEM((2, own_rows, half), bf16),
-            pltpu.VMEM((own_rows, half), f32),
-            pltpu.VMEM((own_rows, half), f32),
-            pltpu.VMEM((own_rows, half), f32),
-            pltpu.VMEM((own_rows, half), f32),
-            dma((6,)), dma((6,)), dma((2,)), dma((3,)), dma((nf,)), dma((nf,)), dma((nf,)), dma((nf,)), dma((nf,)),
-            dma((4,)), dma((4,)), dma((4,)), dma((4,)), dma((2,)), dma((2,)), dma((4, 8)), dma((4, 8)),
+            pltpu.VMEM((chunks, nf, tokens // nf, width), f32),
+            *[pltpu.VMEM((chunks, nf, tokens // nf, width), bf16)] * 3,
+            pltpu.VMEM((chunks, ndp, own_rows, width), f32),
+            pltpu.VMEM((chunks, ndp // 2, own_rows, width), f32),
+            *[pltpu.VMEM((chunks, 2, own_rows, width // 2), bf16)] * 4,
+            *[pltpu.VMEM((chunks, own_rows, width // 2), f32)] * 4,
+            dma((6,)), dma((6,)), dma((2,)), dma((3,)), dma((nf,)), *[dma((chunks, nf))] * 4,
+            *[dma((chunks, 4))] * 4, *[dma((chunks, 2))] * 2, *[dma((3 + chunks, 8))] * 2,
         ],
         compiler_params=pltpu.CompilerParams(
             collective_id=0, has_side_effects=True, vmem_limit_bytes=63 * 1024 * 1024

time: 92.7 us -> 94.2 us (1.016)
  Pallas kernels: 91 us -> 93.4 us
    pallas_call x1, Pallas kernels: 83.5 us -> 85.9 us  [local_fused(): pl.pallas_call(fused_kernel, out_shape=(jax.ShapeDtypeStruct(weight.shape...]
where the time goes in v5:
time: 94.2 us; the launch traced here: 94 us
  Pallas kernels  93.4 us (99%)
    pallas_call x1, Pallas kernels, local_fused(): pl.pallas_call(fused_kernel, out_shape=(jax.ShapeDtypeStruct(weight.shape...  85.9 us
    pallas_call x1, Pallas kernels, local_fused(): pl.pallas_call(store_kernel, out_shape=[jax.ShapeDtypeStruct(r.shape, r.d...  7.52 us

profile of v5, /device:TPU:0, one launch (start us, length us, event | category | flops | bytes accessed | tf_op | source)
XLA Modules:
  0.0 94.0 jit_solution(4966026550716164392)
XLA Ops:
  0.6 85.9 %shard_map.85 = (bf16[1024,4096]{1,0:T(8,128)(2,1)}, f32[128,1024]{1,0:T(8,128)}, f32[128,1024]{1,0:T(8,128)}) custom-call(bf16[256,1024]{1,0:T(8,128)(2,1)} %act_in.1, bf16[256,1024]{1,0:T(8,128)(2,1)} %og_in.1, bf16[8,128,1024]{2,1,0:T(8,128)(2,1)} %bitcast.1, bf16[1024,4096]{1,0:T(8,128)(2,1)} %weight_in.1, f32[128,1024]{1,0:T(8,128)} %first_in.1, ...), custom_call_target="tpu_custom_call" | custom-call | flops 9663676416 | bytes 25165824 | tf_op jit(solution)/shard_map/pallas_call | solution.py:400
  86.5 7.5 %shard_map.86 = (bf16[1024,4096]{1,0:T(8,128)(2,1)}, f32[128,1024]{1,0:T(8,128)}, f32[128,1024]{1,0:T(8,128)}) custom-call(bf16[1024,4096]{1,0:T(8,128)(2,1)} %get-tuple-element.6.weight, f32[128,1024]{1,0:T(8,128)} %get-tuple-element.7.first, f32[128,1024]{1,0:T(8,128)} %get-tuple-element.8.second), custom_call_target="tpu_custom_call" | custom-call | tf_op jit(solution)/shard_map/pallas_call | solution.py:436

commit v6 on v4

--- a/solution.py
+++ b/solution.py
@@ -34,9 +34,9 @@
     weight_out, first_out, second_out,
     act, og, rows, weight, first, second, updates,
     part, part_send, part_recv, proj,
-    grad, grad_core, sa1, sb1, ra1, rb1, sa2, sb2, ra2, rb2,
+    grad, og_sib, proj_sib, sa1, sb1, ra1, rb1, sa2, sb2, ra2, rb2,
     load_sem, store_sem, z_send, z_fwd, z_recv, rs_send, rs_recv, ag_send, ag_recv,
-    core_send, core_recv, h1_send, h1_recv, h2_send, h2_recv, pg_send, pg_recv,
+    core_send, core_recv, og_send, og_recv, h1_send, h1_recv, h2_send, h2_recv, pg_send, pg_recv,
 ):
     i = lax.axis_index("dp")
     j = lax.axis_index("fsdp")
@@ -85,6 +85,9 @@
         pl.semaphore_signal(barrier, inc=1, device_id=(i, (j + d) % nf), device_id_type=MESH)
     pl.semaphore_wait(barrier, 3 + nf - 1)
 
+    mine = 2 * y + x
+    order = (3 - mine, 2 * y + 1 - x, 2 * (1 - y) + x, mine)
+
     def z_piece(shard):
         return rows.at[shard * ndp + i]
 
@@ -95,6 +98,15 @@
     @pl.when(j > 0)
     def _():
         remote(basis_in_ref.at[i], z_piece(j), z_send.at[1], z_recv.at[j], i, j - 1).start()
+
+    def og_columns(k):
+        return pl.ds(pl.multiple_of(k * own_rows, own_rows), own_rows)
+
+    for q in range(4):
+        remote(
+            og_in.at[:, og_columns(2 * order[q] + 1 - core)], og_sib.at[q],
+            og_send.at[q], og_recv.at[q], sib, j,
+        ).start()
 
     loads[0].wait()
     loads[1].wait()
@@ -193,6 +205,7 @@
     for d in (1, 2, 3):
         z = (j + d) % nf
         remote(proj.at[j], proj.at[j], ag_send.at[z], ag_recv.at[j], i, z).start()
+    remote(proj.at[j], proj_sib.at[j], core_send.at[j], core_recv.at[j], sib, j).start()
 
     stage2(rows, shard_of(0) * ndp, 0)
     basis_in(2)
@@ -202,43 +215,31 @@
     for d in (1, 2, 3):
         z = (j + d) % nf
         got(proj.at[z], ag_recv.at[z], ag_send.at[z])
+        remote(proj.at[z], proj_sib.at[z], core_send.at[z], core_recv.at[z], sib, j).start()
 
     loads[2].wait()
     projected = proj[...].reshape(tokens, rank)
 
-    def term(k):
-        cols = pl.ds(pl.multiple_of(k * own_rows, own_rows), own_rows)
-        return lax.dot_general(
-            og[:, cols], projected, (((0,), (0,)), ((), ())), preferred_element_type=f32
-        )
-
-    mine = 2 * y + x
-    order = (3 - mine, 2 * y + 1 - x, 2 * (1 - y) + x, mine)
+    def over_tokens(left, right):
+        return lax.dot_general(left, right, (((0,), (0,)), ((), ())), preferred_element_type=f32)
+
     for q in range(4):
-        grad[4 + q] = term(2 * order[q] + 1 - core)
-        remote(grad.at[4 + q], grad_core.at[q], core_send.at[q], core_recv.at[q], sib, j).start()
+        grad[q] = over_tokens(og[:, og_columns(2 * order[q] + core)], projected)
     for q in range(4):
-        grad[q] = term(2 * order[q] + core)
-
-    def pair_sum(q):
-        got(grad_core.at[q], core_recv.at[q], core_send.at[q])
-        grad[q] = grad[q] + grad_core[q]
-
-    def hop1(n, qa, qb):
-        if qa is not None:
-            sa1[n] = grad[qa, :, 0:half].astype(bf16)
-            remote(sa1.at[n], ra1.at[n], h1_send.at[n], h1_recv.at[n], xn, j).start()
-        if qb is not None:
-            sb1[n] = grad[qb, :, half:rank].astype(bf16)
+        got(og_sib.at[q], og_recv.at[q], og_send.at[q])
+    for z in range(nf):
+        got(proj_sib.at[z], core_recv.at[z], core_send.at[z])
+    projected_sib = proj_sib[...].reshape(tokens, rank)
+
+    for q in range(4):
+        grad[q] = grad[q] + over_tokens(og_sib[q], projected_sib)
+        if q in (0, 1):
+            sa1[q] = grad[q, :, 0:half].astype(bf16)
+            remote(sa1.at[q], ra1.at[q], h1_send.at[q], h1_recv.at[q], xn, j).start()
+        if q in (0, 2):
+            n = q // 2
+            sb1[n] = grad[q, :, half:rank].astype(bf16)
             remote(sb1.at[n], rb1.at[n], h1_send.at[2 + n], h1_recv.at[2 + n], yn, j).start()
-
-    pair_sum(0)
-    hop1(0, 0, 0)
-    pair_sum(1)
-    hop1(1, 1, None)
-    pair_sum(2)
-    hop1(1, None, 2)
-    pair_sum(3)
     stage3(rows, shard_of(1) * ndp, 1)
     stage2(rows, shard_of(2) * ndp, 2)
     got(ra1.at[0], h1_recv.at[0], h1_send.at[0])
@@ -320,7 +321,8 @@
         sent(part_send.at[z], rs_send.at[z], rs_recv.at[z])
         sent(proj.at[j], ag_send.at[z], ag_recv.at[z])
     for q in range(4):
-        sent(grad.at[4 + q], core_send.at[q], core_recv.at[q])
+        sent(proj.at[q], core_send.at[q], core_recv.at[q])
+        sent(og_sib.at[q], og_send.at[q], og_recv.at[q])
     for n in range(2):
         sent(sa1.at[n], h1_send.at[n], h1_recv.at[n])
         sent(sb1.at[n], h1_send.at[2 + n], h1_recv.at[2 + n])
@@ -384,8 +386,9 @@
             pltpu.VMEM((nf, tokens // nf, rank), bf16),
             pltpu.VMEM((nf, tokens // nf, rank), bf16),
             pltpu.VMEM((nf, tokens // nf, rank), bf16),
-            pltpu.VMEM((ndp, own_rows, rank), f32),
             pltpu.VMEM((ndp // 2, own_rows, rank), f32),
+            pltpu.VMEM((ndp // 2, tokens, own_rows), bf16),
+            pltpu.VMEM((nf, tokens // nf, rank), bf16),
             pltpu.VMEM((2, own_rows, half), bf16),
             pltpu.VMEM((2, own_rows, half), bf16),
             pltpu.VMEM((2, own_rows, half), bf16),
@@ -395,7 +398,7 @@
             pltpu.VMEM((own_rows, half), f32),
             pltpu.VMEM((own_rows, half), f32),
             dma((6,)), dma((6,)), dma((2,)), dma((3,)), dma((nf,)), dma((nf,)), dma((nf,)), dma((nf,)), dma((nf,)),
-            dma((4,)), dma((4,)), dma((4,)), dma((4,)), dma((2,)), dma((2,)), dma((4, 8)), dma((4, 8)),
+            *[dma((4,))] * 6, dma((2,)), dma((2,)), dma((4, 8)), dma((4, 8)),
         ],
         compiler_params=pltpu.CompilerParams(
             collective_id=0, has_side_effects=True, vmem_limit_bytes=63 * 1024 * 1024

time: 92.7 us -> 92.7 us (level)
  no operation moved by 1% of the time
where the time goes in v6:
time: 92.7 us; the launch traced here: 91.7 us
  Pallas kernels  91 us (98%)
    pallas_call x1, Pallas kernels, local_fused(): pl.pallas_call(fused_kernel, out_shape=(jax.ShapeDtypeStruct(weight.shape...  83.5 us
    pallas_call x1, Pallas kernels, local_fused(): pl.pallas_call(store_kernel, out_shape=[jax.ShapeDtypeStruct(r.shape, r.d...  7.52 us

profile of v6, /device:TPU:0, one launch (start us, length us, event | category | flops | bytes accessed | tf_op | source)
XLA Modules:
  0.0 91.7 jit_solution(2022156784726360891)
XLA Ops:
  0.6 83.5 %shard_map.85 = (bf16[1024,4096]{1,0:T(8,128)(2,1)}, f32[128,1024]{1,0:T(8,128)}, f32[128,1024]{1,0:T(8,128)}) custom-call(bf16[256,1024]{1,0:T(8,128)(2,1)} %act_in.1, bf16[256,1024]{1,0:T(8,128)(2,1)} %og_in.1, bf16[8,128,1024]{2,1,0:T(8,128)(2,1)} %bitcast.1, bf16[1024,4096]{1,0:T(8,128)(2,1)} %weight_in.1, f32[128,1024]{1,0:T(8,128)} %first_in.1, ...), custom_call_target="tpu_custom_call" | custom-call | flops 9663676416 | bytes 25165824 | tf_op jit(solution)/shard_map/pallas_call | solution.py:368
  84.2 7.5 %shard_map.86 = (bf16[1024,4096]{1,0:T(8,128)(2,1)}, f32[128,1024]{1,0:T(8,128)}, f32[128,1024]{1,0:T(8,128)}) custom-call(bf16[1024,4096]{1,0:T(8,128)(2,1)} %get-tuple-element.6.weight, f32[128,1024]{1,0:T(8,128)} %get-tuple-element.7.first, f32[128,1024]{1,0:T(8,128)} %get-tuple-element.8.second), custom_call_target="tpu_custom_call" | custom-call | tf_op jit(solution)/shard_map/pallas_call | solution.py:413

commit v7 on v6

--- a/solution.py
+++ b/solution.py
@@ -117,9 +117,10 @@
     )
     part[...] = acc.reshape(nf, tb, rank)
     part_send[...] = acc.reshape(nf, tb, rank).astype(bf16)
-    for d in (1, 2, 3):
-        z = (j + d) % nf
-        remote(part_send.at[z], part_recv.at[j], rs_send.at[z], rs_recv.at[j], i, z).start()
+    def scatter():
+        for d in (2, 1, 3):
+            z = (j + d) % nf
+            remote(part_send.at[z], part_recv.at[j], rs_send.at[z], rs_recv.at[j], i, z).start()
 
     def block(buf, base, k):
         return buf.at[base + k]
@@ -193,8 +194,21 @@
         def _():
             sent(z_piece(s), z_fwd.at[g], z_recv.at[s])
 
+    middle = (j > 0) & (j < nf - 1)
+
+    @pl.when(jnp.logical_not(middle))
+    def _():
+        scatter()
+
     basis_in(0)
     basis_in(1)
+
+    @pl.when(middle)
+    def _():
+        scatter()
+        basis_in(2)
+
+    stage2(rows, shard_of(0) * ndp, 0)
 
     total = part[j]
     for d in (1, 2, 3):
@@ -207,8 +221,10 @@
         remote(proj.at[j], proj.at[j], ag_send.at[z], ag_recv.at[j], i, z).start()
     remote(proj.at[j], proj_sib.at[j], core_send.at[j], core_recv.at[j], sib, j).start()
 
-    stage2(rows, shard_of(0) * ndp, 0)
-    basis_in(2)
+    @pl.when(jnp.logical_not(middle))
+    def _():
+        basis_in(2)
+
     stage3(rows, shard_of(0) * ndp, 0)
     stage2(rows, shard_of(1) * ndp, 1)
 
@@ -225,6 +241,8 @@
 
     for q in range(4):
         grad[q] = over_tokens(og[:, og_columns(2 * order[q] + core)], projected)
+    stage3(rows, shard_of(1) * ndp, 1)
+    stage2(rows, shard_of(2) * ndp, 2)
     for q in range(4):
         got(og_sib.at[q], og_recv.at[q], og_send.at[q])
     for z in range(nf):
@@ -240,8 +258,6 @@
             n = q // 2
             sb1[n] = grad[q, :, half:rank].astype(bf16)
             remote(sb1.at[n], rb1.at[n], h1_send.at[2 + n], h1_recv.at[2 + n], yn, j).start()
-    stage3(rows, shard_of(1) * ndp, 1)
-    stage2(rows, shard_of(2) * ndp, 2)
     got(ra1.at[0], h1_recv.at[0], h1_send.at[0])
     sa2[...] = grad[2, :, 0:half] + ra1[0].astype(f32)
     remote(sa2, ra2, h2_send.at[0], h2_recv.at[0], yn, j).start()

time: 92.7 us -> 92.9 us (level)
  Pallas kernels: 91 us -> 92.1 us
    pallas_call x1, Pallas kernels: 83.5 us -> 84.6 us  [local_fused(): pl.pallas_call(fused_kernel, out_shape=(jax.ShapeDtypeStruct(weight.shape...]
where the time goes in v7:
time: 92.9 us; the launch traced here: 92.8 us
  Pallas kernels  92.1 us (99%)
    pallas_call x1, Pallas kernels, local_fused(): pl.pallas_call(fused_kernel, out_shape=(jax.ShapeDtypeStruct(weight.shape...  84.6 us
    pallas_call x1, Pallas kernels, local_fused(): pl.pallas_call(store_kernel, out_shape=[jax.ShapeDtypeStruct(r.shape, r.d...  7.52 us

profile of v7, /device:TPU:0, one launch (start us, length us, event | category | flops | bytes accessed | tf_op | source)
XLA Modules:
  0.0 92.8 jit_solution(4242707931316290024)
XLA Ops:
  0.6 84.6 %shard_map.85 = (bf16[1024,4096]{1,0:T(8,128)(2,1)}, f32[128,1024]{1,0:T(8,128)}, f32[128,1024]{1,0:T(8,128)}) custom-call(bf16[256,1024]{1,0:T(8,128)(2,1)} %act_in.1, bf16[256,1024]{1,0:T(8,128)(2,1)} %og_in.1, bf16[8,128,1024]{2,1,0:T(8,128)(2,1)} %bitcast.1, bf16[1024,4096]{1,0:T(8,128)(2,1)} %weight_in.1, f32[128,1024]{1,0:T(8,128)} %first_in.1, ...), custom_call_target="tpu_custom_call" | custom-call | flops 9663676416 | bytes 25165824 | tf_op jit(solution)/shard_map/pallas_call | solution.py:384
  85.3 7.5 %shard_map.86 = (bf16[1024,4096]{1,0:T(8,128)(2,1)}, f32[128,1024]{1,0:T(8,128)}, f32[128,1024]{1,0:T(8,128)}) custom-call(bf16[1024,4096]{1,0:T(8,128)(2,1)} %get-tuple-element.6.weight, f32[128,1024]{1,0:T(8,128)} %get-tuple-element.7.first, f32[128,1024]{1,0:T(8,128)} %get-tuple-element.8.second), custom_call_target="tpu_custom_call" | custom-call | tf_op jit(solution)/shard_map/pallas_call | solution.py:429

commit v8 on v5

--- a/solution.py
+++ b/solution.py
@@ -34,9 +34,9 @@
     weight_out, first_out, second_out,
     act, og, rows, weight, first, second, updates,
     part, part_send, part_recv, proj,
-    grad, grad_core, sa1, sb1, ra1, rb1, sa2, sb2, ra2, rb2,
+    grad, og_sib, proj_sib, sa1, sb1, ra1, rb1, sa2, sb2, ra2, rb2,
     load_sem, store_sem, z_send, z_fwd, z_recv, rs_send, rs_recv, ag_send, ag_recv,
-    core_send, core_recv, h1_send, h1_recv, h2_send, h2_recv, pg_send, pg_recv,
+    core_send, core_recv, og_send, og_recv, h1_send, h1_recv, h2_send, h2_recv, pg_send, pg_recv,
 ):
     i = lax.axis_index("dp")
     j = lax.axis_index("fsdp")
@@ -87,6 +87,9 @@
         pl.semaphore_signal(barrier, inc=1, device_id=(i, (j + d) % nf), device_id_type=MESH)
     pl.semaphore_wait(barrier, 3 + nf - 1)
 
+    mine = 2 * y + x
+    order = (3 - mine, 2 * y + 1 - x, 2 * (1 - y) + x, mine)
+
     def z_piece(shard):
         return rows.at[shard * ndp + i]
 
@@ -97,6 +100,15 @@
     @pl.when(j > 0)
     def _():
         remote(basis_in_ref.at[i], z_piece(j), z_send.at[1], z_recv.at[j], i, j - 1).start()
+
+    def og_columns(k):
+        return pl.ds(pl.multiple_of(k * own_rows, own_rows), own_rows)
+
+    for q in range(4):
+        remote(
+            og_in.at[:, og_columns(2 * order[q] + 1 - core)], og_sib.at[q],
+            og_send.at[q], og_recv.at[q], sib, j,
+        ).start()
 
     loads[0].wait()
     loads[1].wait()
@@ -114,6 +126,11 @@
         for d in (2, 1, 3):
             z = (j + d) % nf
             remote(part_send.at[c, z], part_recv.at[c, j], rs_send.at[c, z], rs_recv.at[c, j], i, z).start()
+
+    def to_sibling(c, z):
+        remote(
+            proj.at[c, z], proj_sib.at[c, z], core_send.at[c, z], core_recv.at[c, z], sib, j
+        ).start()
 
     def reduce_gather(c):
         total = part[c, j]
@@ -125,10 +142,9 @@
         for d in (2, 1, 3):
             z = (j + d) % nf
             remote(proj.at[c, j], proj.at[c, j], ag_send.at[c, z], ag_recv.at[c, j], i, z).start()
-
-    partial(0)
-    scatter(0)
-    for c in range(1, chunks):
+        to_sibling(c, j)
+
+    for c in range(chunks):
         partial(c)
 
     def columns(g, base, k, start, stop):
@@ -208,33 +224,22 @@
         def _():
             sent(z_piece(s), z_fwd.at[g], z_recv.at[s])
 
-    mine = 2 * y + x
-    order = (3 - mine, 2 * y + 1 - x, 2 * (1 - y) + x, mine)
+    def over_tokens(left, right):
+        return lax.dot_general(left, right, (((0,), (0,)), ((), ())), preferred_element_type=f32)
 
     def low_grad(c):
         for d in (1, 2, 3):
             z = (j + d) % nf
             got(proj.at[c, z], ag_recv.at[c, z], ag_send.at[c, z])
+            to_sibling(c, z)
         projected = proj[c].reshape(tokens, width)
-
-        def term(k):
-            cols = pl.ds(pl.multiple_of(k * own_rows, own_rows), own_rows)
-            return lax.dot_general(
-                og[:, cols], projected, (((0,), (0,)), ((), ())), preferred_element_type=f32
-            )
-
         for q in range(4):
-            grad[c, 4 + q] = term(2 * order[q] + 1 - core)
-            remote(
-                grad.at[c, 4 + q], grad_core.at[c, q], core_send.at[c, q], core_recv.at[c, q], sib, j
-            ).start()
+            grad[c, q] = over_tokens(og[:, og_columns(2 * order[q] + core)], projected)
+        for z in range(nf):
+            got(proj_sib.at[c, z], core_recv.at[c, z], core_send.at[c, z])
+        projected_sib = proj_sib[c].reshape(tokens, width)
         for q in range(4):
-            grad[c, q] = term(2 * order[q] + core)
-
-    def hop1(c):
-        for q in range(4):
-            got(grad_core.at[c, q], core_recv.at[c, q], core_send.at[c, q])
-            grad[c, q] = grad[c, q] + grad_core[c, q]
+            grad[c, q] = grad[c, q] + over_tokens(og_sib[q], projected_sib)
             if q in (0, 1):
                 sa1[c, q] = grad[c, q, :, 0:lane].astype(bf16)
                 remote(sa1.at[c, q], ra1.at[c, q], h1_send.at[c, q], h1_recv.at[c, q], xn, j).start()
@@ -265,35 +270,40 @@
 
     middle = (j > 0) & (j < nf - 1)
     shard_base = [shard_of(g) * ndp for g in range(3)]
+    @pl.when(jnp.logical_not(middle))
+    def _():
+        scatter(0)
+
     basis_in(0)
+    basis_in(1)
+
+    @pl.when(middle)
+    def _():
+        scatter(0)
+        basis_in(2)
+
+    stage2(shard_base[0], 0)
     reduce_gather(0)
     scatter(1)
-    basis_in(1)
-    stage2(shard_base[0], 0)
-
-    @pl.when(middle)
+
+    @pl.when(jnp.logical_not(middle))
     def _():
         basis_in(2)
 
+    stage3(shard_base[0], 0)
+    stage2(shard_base[1], 1)
     reduce_gather(1)
     loads[2].wait()
+    for q in range(4):
+        got(og_sib.at[q], og_recv.at[q], og_send.at[q])
     low_grad(0)
-    hop1(0)
-    stage3(shard_base[0], 0)
-    stage2(shard_base[1], 1)
+    stage3(shard_base[1], 1)
+    stage2(shard_base[2], 2)
     hop2(0)
-
-    @pl.when(jnp.logical_not(middle))
-    def _():
-        basis_in(2)
-
     low_grad(1)
     loads[3].wait()
     loads[4].wait()
     step(0)
-    hop1(1)
-    stage3(shard_base[1], 1)
-    stage2(shard_base[2], 2)
     hop2(1)
     stage2(0, 3)
     stage3(shard_base[2], 2)
@@ -353,12 +363,14 @@
             sent(part_send.at[c, z], rs_send.at[c, z], rs_recv.at[c, z])
             sent(proj.at[c, j], ag_send.at[c, z], ag_recv.at[c, z])
         for q in range(4):
-            sent(grad.at[c, 4 + q], core_send.at[c, q], core_recv.at[c, q])
+            sent(proj.at[c, q], core_send.at[c, q], core_recv.at[c, q])
         for n in range(2):
             sent(sa1.at[c, n], h1_send.at[c, n], h1_recv.at[c, n])
             sent(sb1.at[c, n], h1_send.at[c, 2 + n], h1_recv.at[c, 2 + n])
         sent(sa2.at[c], h2_send.at[c, 0], h2_recv.at[c, 0])
         sent(sb2.at[c], h2_send.at[c, 1], h2_recv.at[c, 1])
+    for q in range(4):
+        sent(og_sib.at[q], og_send.at[q], og_recv.at[q])
     store_first.wait()
     store_second.wait()
     for n, o in enumerate((i, xn, yn, dn)):
@@ -416,12 +428,13 @@
             pltpu.VMEM((ndp, own_rows, rank), bf16),
             pltpu.VMEM((chunks, nf, tokens // nf, width), f32),
             *[pltpu.VMEM((chunks, nf, tokens // nf, width), bf16)] * 3,
-            pltpu.VMEM((chunks, ndp, own_rows, width), f32),
             pltpu.VMEM((chunks, ndp // 2, own_rows, width), f32),
+            pltpu.VMEM((ndp // 2, tokens, own_rows), bf16),
+            pltpu.VMEM((chunks, nf, tokens // nf, width), bf16),
             *[pltpu.VMEM((chunks, 2, own_rows, width // 2), bf16)] * 4,
             *[pltpu.VMEM((chunks, own_rows, width // 2), f32)] * 4,
             dma((6,)), dma((6,)), dma((2,)), dma((3,)), dma((nf,)), *[dma((chunks, nf))] * 4,
-            *[dma((chunks, 4))] * 4, *[dma((chunks, 2))] * 2, *[dma((3 + chunks, 8))] * 2,
+            *[dma((chunks, 4))] * 2, *[dma((4,))] * 2, *[dma((chunks, 4))] * 2, *[dma((chunks, 2))] * 2, *[dma((3 + chunks, 8))] * 2,
         ],
         compiler_params=pltpu.CompilerParams(
             collective_id=0, has_side_effects=True, vmem_limit_bytes=63 * 1024 * 1024

time: 94.2 us -> 89.7 us (0.952)
  Pallas kernels: 93.4 us -> 88.8 us
    pallas_call x1, Pallas kernels: 85.9 us -> 81.3 us  [local_fused(): pl.pallas_call(fused_kernel, out_shape=(jax.ShapeDtypeStruct(weight.shape...]
where the time goes in v8:
time: 89.7 us; the launch traced here: 89.5 us
  Pallas kernels  88.8 us (99%)
    pallas_call x1, Pallas kernels, local_fused(): pl.pallas_call(fused_kernel, out_shape=(jax.ShapeDtypeStruct(weight.shape...  81.3 us
    pallas_call x1, Pallas kernels, local_fused(): pl.pallas_call(store_kernel, out_shape=[jax.ShapeDtypeStruct(r.shape, r.d...  7.52 us

profile of v8, /device:TPU:0, one launch (start us, length us, event | category | flops | bytes accessed | tf_op | source)
XLA Modules:
  0.0 89.5 jit_solution(14053319019690689088)
XLA Ops:
  0.6 81.3 %shard_map.85 = (bf16[1024,4096]{1,0:T(8,128)(2,1)}, f32[128,1024]{1,0:T(8,128)}, f32[128,1024]{1,0:T(8,128)}) custom-call(bf16[256,1024]{1,0:T(8,128)(2,1)} %act_in.1, bf16[256,1024]{1,0:T(8,128)(2,1)} %og_in.1, bf16[8,128,1024]{2,1,0:T(8,128)(2,1)} %bitcast.1, bf16[1024,4096]{1,0:T(8,128)(2,1)} %weight_in.1, f32[128,1024]{1,0:T(8,128)} %first_in.1, ...), custom_call_target="tpu_custom_call" | custom-call | flops 9663676416 | bytes 25165824 | tf_op jit(solution)/shard_map/pallas_call | solution.py:412
  81.9 7.5 %shard_map.86 = (bf16[1024,4096]{1,0:T(8,128)(2,1)}, f32[128,1024]{1,0:T(8,128)}, f32[128,1024]{1,0:T(8,128)}) custom-call(bf16[1024,4096]{1,0:T(8,128)(2,1)} %get-tuple-element.6.weight, f32[128,1024]{1,0:T(8,128)} %get-tuple-element.7.first, f32[128,1024]{1,0:T(8,128)} %get-tuple-element.8.second), custom_call_target="tpu_custom_call" | custom-call | tf_op jit(solution)/shard_map/pallas_call | solution.py:449
